TPU v7x, 512 devices: a whole 4x4x16 slice. The times are simulated.
512 devices in a mesh: samp: 32 (over z, core), state: 16 (over x, y).
Axes of the slice: x: 4, y: 4, z: 16, core: 2. Of those that a mesh axis runs over, the one named last changes fastest.
Arguments:
- energies: float32 [16384, 64, 256], P(('samp', 'state')), may hold values from -170 to 90, as said below
- tile_rows: int32 [16384], P(('samp', 'state')), may hold values from 0 to 63, as said below
- tile_cols: int32 [16384], P(('samp', 'state')), may hold values from 0 to 16, as said below
- start_free: float32 [16384], P('state'), may hold values from -8 to 8
- temps: int32 [16384], P('state'), may hold values from 0 to 15
- betas: float32 [16], replicated, may hold values from 0.4 to 2.5
- counts: int32 [16384], P('state'), may hold values from 256 to 768
- basis: bfloat16 [32, 524288], P(None, 'samp'), may hold values from -6 to 6
Outputs:
- averages: float32 [32, 16384], P(None, 'state')
Inputs may be any that keep to these rules, and one draw needn't show every extreme that they name: `tile_cols`: empty slots hold 16. On each device the live slots come first, their (row, column) pairs are distinct, and the live count lies between 1 and 32; in every column of devices along samp one device has all 32 slots live and covers each of its 16 state blocks. `tile_rows`: 0 on empty slots. `energies`: values of empty slots are arbitrary.
All inputs are finite; a program needn't handle non-finite values.
Results may differ from a plain program's by a relative error of at most 0.0003.
Values sent between devices are 32-bit elements; how exact they have to be, the bound alone decides.
No kernel may reach another device: no remote copies, remote signals or barrier semaphores. Data moves between devices by JAX's collectives and lax.ppermute only.
A program may use at most 64 MiB of HBM per device.

v0:
```python
import jax
import jax.numpy as jnp
from jax import lax
from jax.sharding import PartitionSpec as P

ITERS = 2


NEG = -1e30


def combined_all(value, axis, join):
    pieces = jax.tree.map(lambda part: lax.all_gather(part, axis), value)
    head = jax.tree.map(lambda part: part[0], pieces)
    tail = jax.tree.map(lambda part: part[1:], pieces)
    subtotal, _ = lax.scan(lambda subtotal, piece: (join(subtotal, piece), None), head, tail)
    return subtotal


def combine_pairs(first, second):
    peak = jnp.maximum(first[0], second[0])
    left = jnp.exp(first[0] - peak)
    right = jnp.exp(second[0] - peak)
    return (peak,) + tuple((a * left + b * right for a, b in zip(first[1:], second[1:])))


def on_device(energies, tile_rows, tile_cols, start_free, temps, betas, counts, basis):
    state_block = energies.shape[1]
    sample_block = energies.shape[2]
    state_dev = start_free.shape[0]
    blocks_state = state_dev // state_block
    blocks_samp = basis.shape[1] // sample_block
    live = tile_cols < blocks_state
    cols = jnp.minimum(tile_cols, blocks_state - 1)
    row_hot = (tile_rows[None, :] == jnp.arange(blocks_samp)[:, None]) & live[None, :]
    col_hot = tile_cols[None, :] == jnp.arange(blocks_state)[:, None]
    row_float = row_hot.astype(jnp.float32)
    col_float = col_hot.astype(jnp.float32)
    temp_hot = temps[:, None] == jnp.arange(betas.shape[0])[None, :]
    beta_state = jnp.sum(jnp.where(temp_hot, betas[None, :], 0.0), axis=1)
    reduced = beta_state.reshape(blocks_state, state_block)[cols][:, :, None] * energies
    log_count = jnp.log(counts.astype(jnp.float32))
    free = start_free
    averages = None
    for step in range(ITERS):
        bias = (log_count + free).reshape(blocks_state, state_block)[cols]
        score = jnp.where(live[:, None, None], bias[:, :, None] - reduced, NEG)
        tile_peak = jnp.max(score, axis=1)
        block_peak = jnp.max(jnp.where(row_hot[:, :, None], tile_peak[None], NEG), axis=1)
        shift = block_peak[tile_rows]
        tile_total = jnp.sum(jnp.exp(score - shift[:, None, :]), axis=1)
        block_total = jnp.dot(row_float, tile_total, precision=lax.Precision.HIGHEST)
        local_peak = block_peak.reshape(-1)
        local_total = block_total.reshape(-1)
        peak = lax.pmax(local_peak, "state")
        total = lax.psum(local_total * jnp.exp(local_peak - peak), "state")
        drop = (peak + jnp.log(jnp.maximum(total, 1.0))).reshape(blocks_samp, sample_block)
        drop_tile = drop[tile_rows]
        value = jnp.where(live[:, None, None], -reduced - drop_tile[:, None, :], NEG)
        peak_tile = jnp.max(value, axis=2)
        state_peak = jnp.max(jnp.where(col_hot[:, :, None], peak_tile[None], NEG), axis=1)
        weight = jnp.exp(value - state_peak[cols][:, :, None])
        state_total = jnp.dot(
            col_float, jnp.sum(weight, axis=2), precision=lax.Precision.HIGHEST
        ).reshape(-1)
        state_top = state_peak.reshape(-1)
        if step + 1 < ITERS:
            top, whole = combined_all((state_top, state_total), "samp", combine_pairs)
            free = -(top + jnp.log(whole))
        else:
            values = basis.reshape(basis.shape[0], blocks_samp, sample_block)[:, tile_rows].astype(
                jnp.float32
            )
            tile_numer = jnp.einsum("tab,mtb->mta", weight, values, precision=lax.Precision.HIGHEST)
            state_numer = jnp.einsum(
                "kt,mta->mka", col_float, tile_numer, precision=lax.Precision.HIGHEST
            ).reshape(basis.shape[0], state_dev)
            top, whole, numer = combined_all(
                (state_top, state_total, state_numer), "samp", combine_pairs
            )
            averages = numer / whole[None, :]
    return averages


def solution(mesh):
    return jax.shard_map(
        on_device,
        mesh=mesh,
        in_specs=(
            P(("samp", "state"), None, None),
            P(("samp", "state")),
            P(("samp", "state")),
            P("state"),
            P("state"),
            P(),
            P("state"),
            P(None, "samp"),
        ),
        out_specs=P(None, "state"),
        check_vma=False,
    )
```

profile of v0, /device:TPU:1, one launch (start us, length us, event | category | flops | bytes accessed | tf_op | source)
XLA Modules:
  0.0 664.9 jit_solution(13084004217319927948)
XLA Ops:
  6.5 0.8 compare_select_fusion.1
  8.0 0.8 select_reduce_fusion.4
  8.9 0.7 fusion.23
  11.5 2.0 fusion.1
  15.5 0.8 exponential_reduce_fusion.2
  16.5 113.9 %all-reduce.5.cloned.1.call-done = f32[16384]{0:T(1024)} async-done(((f32[16384]{0:T(1024)}), f32[16384]{0:T(1024)}) %all-reduce.5.cloned.1.call-update) | async-done | bytes 65552 | tf_op jit(solution)/shard_map/pmax | solution.py:55
  130.4 1.5 exponential_multiply_fusion.1
  132.0 113.1 %all-reduce.7.cloned.1.call-done = f32[16384]{0:T(1024)} async-done(((f32[16384]{0:T(1024)}), f32[16384]{0:T(1024)}) %all-reduce.7.cloned.1.call-update) | async-done | bytes 65552 | tf_op jit(solution)/shard_map/psum | solution.py:56
  245.2 0.9 log_add_fusion.1
  246.7 0.8 fusion.5
  248.3 1.1 exponential_reduce_fusion.1
  249.7 33.4 %all-gather.1 = f32[32,1,1024]{2,1,0:T(1,128)S(1)} all-gather(f32[1,1,1024]{2,1,0:T(1,128)S(1)} %reshape.199), channel_id=1, replica_groups=mesh['samp'=32,'state'=16] {'samp'}, dimensions={0}, use_global_device_ids=true | all-gather | bytes 135168 | tf_op jit(solution)/shard_map/all_gather | solution.py:13
  283.1 28.5 %all-gather = f32[32,1,1024]{2,1,0:T(1,128)S(1)} all-gather(f32[1,1,1024]{2,1,0:T(1,128)S(1)} %reshape.197), channel_id=1, replica_groups=mesh['samp'=32,'state'=16] {'samp'}, dimensions={0}, use_global_device_ids=true | all-gather | bytes 135168 | tf_op jit(solution)/shard_map/all_gather | solution.py:13
  311.7 1.7 while.26
  314.0 0.8 fusion.2
  316.0 0.8 exponential_reduce_fusion
  317.8 105.5 %all-reduce.9.cloned.1.call-done = f32[16384]{0:T(1024)} async-done(((f32[16384]{0:T(1024)}), f32[16384]{0:T(1024)}) %all-reduce.9.cloned.1.call-update) | async-done | bytes 65552 | tf_op jit(solution)/shard_map/pmax | solution.py:55
  423.3 1.6 exponential_multiply_fusion
  424.9 1.4 copy.43
  426.3 1.4 gather_fusion.9
  427.6 110.2 %all-reduce.11.cloned.1.call-done = f32[16384]{0:T(1024)} async-done(((f32[16384]{0:T(1024)}), f32[16384]{0:T(1024)}) %all-reduce.11.cloned.1.call-update) | async-done | bytes 65552 | tf_op jit(solution)/shard_map/psum | solution.py:56
  537.8 0.9 log_add_fusion
  539.3 0.8 fusion.6
  540.8 2.3 fusion.7
  543.8 0.8 all_gather_reshape.19
  544.7 1.1 fusion.4
  546.0 33.4 %all-gather.3 = f32[32,1,1024]{2,1,0:T(1,128)S(1)} all-gather(f32[1,1,1024]{2,1,0:T(1,128)S(1)} %reshape.203), channel_id=1, replica_groups=mesh['samp'=32,'state'=16] {'samp'}, dimensions={0}, use_global_device_ids=true | all-gather | bytes 135168 | tf_op jit(solution)/shard_map/all_gather | solution.py:13
  579.5 28.5 %all-gather.2 = f32[32,1,1024]{2,1,0:T(1,128)S(1)} all-gather(f32[1,1,1024]{2,1,0:T(1,128)S(1)} %reshape.201), channel_id=1, replica_groups=mesh['samp'=32,'state'=16] {'samp'}, dimensions={0}, use_global_device_ids=true | all-gather | bytes 135168 | tf_op jit(solution)/shard_map/all_gather | solution.py:13
  608.1 12.4 %all-gather.6.cloned.1.call-done = f32[32,32,1024]{2,1,0:T(8,128)} async-done(((f32[1,32,1024]{2,1,0:T(8,128)}), f32[32,32,1024]{2,1,0:T(8,128)}) %all-gather.6.cloned.1.call-update) | async-done | bytes 4194320 | tf_op jit(solution)/shard_map/all_gather | solution.py:13
  620.4 4.6 slice.77
  625.1 0.9 slice_bitcast_fusion
  626.0 31.7 %while.27 = (s32[]{:T(128)}, f32[1024]{0:T(1024)S(1)}, f32[1024]{0:T(1024)S(1)}, f32[32,1024]{1,0:T(8,128)S(1)}, f32[31,1024]{1,0:T(8,128)S(1)}, /*index=5*/f32[...) while((s32[]{:T(128)}, f32[1024]{0:T(1024)S(1)}, f32[1024]{0:T(1024)S(1)}, f32[32,1024]{1,0:T(8,128)S(1)}, ...), condition=%wide.region_20.21_spmd, body=%wide.region_19.20_spmd.sunk | while | flops 104450 | bytes 450653 | solution.py:16
  626.0 1.0 fusion.32
  627.0 1.0 fusion.32
  628.1 1.0 fusion.32
  629.1 1.0 fusion.32
  630.1 1.0 fusion.32
  631.1 1.0 fusion.32
  632.2 1.0 fusion.32
  633.2 1.0 fusion.32
  634.2 1.0 fusion.32
  635.2 1.0 fusion.32
  636.2 1.0 fusion.32
  637.3 1.0 fusion.32
  638.3 1.0 fusion.32
  639.3 1.0 fusion.32
  640.3 1.0 fusion.32
  641.4 1.0 fusion.32
  642.4 1.0 fusion.32
  643.4 1.0 fusion.32
  644.4 1.0 fusion.32
  645.5 1.0 fusion.32
  646.5 1.0 fusion.32
  647.5 1.0 fusion.32
  648.5 1.0 fusion.32
  649.5 1.0 fusion.32
  650.6 1.0 fusion.32
  651.6 1.0 fusion.32
  652.6 1.0 fusion.32
  653.6 1.0 fusion.32
  654.7 1.0 fusion.32
  655.7 1.0 fusion.32
  656.7 1.0 fusion.32
  657.7 0.7 broadcast_divide_fusion
  (198 shorter events, 13.3 us)
Async XLA Ops:
  6.5 8.3 %copy-start.6 = (s32[32]{0:T(128)S(1)}, s32[32]{0:T(128)}, u32[]{:S(2)}) copy-start(s32[32]{0:T(128)} %param.13) | copy-start | bytes 388
  6.5 8.9 %copy-start = (f32[32,64,256]{2,1,0:T(8,128)S(1)}, f32[32,64,256]{2,1,0:T(8,128)}, u32[]{:S(2)}) copy-start(f32[32,64,256]{2,1,0:T(8,128)} %param.12) | copy-start | bytes 6291460
  6.5 123.9 %all-reduce.5.cloned.1.call-start = ((), (), s32[]{:S(2)}) async-start(), calls=%async_computation | async-start | bytes 131072 | tf_op jit(solution)/shard_map/pmax | solution.py:55
  13.5 118.5 %copy-start.5 = (s32[32]{0:T(128)S(1)}, s32[32]{0:T(128)}, u32[]{:S(2)}) copy-start(s32[32]{0:T(128)} %param.14) | copy-start | bytes 388
  14.7 115.7 %copy-start.1 = (f32[8,2,8,128]{3,1,2,0:T(2,128)S(1)}, f32[8,2,8,128]{3,1,2,0:T(2,128)}, u32[]{:S(2)}) copy-start(f32[8,2,8,128]{3,1,2,0:T(2,128)} %copy.32) | copy-start | bytes 196612
  14.8 230.4 %all-reduce.7.cloned.1.call-start = ((), (), s32[]{:S(2)}) async-start(), calls=%async_computation.1 | async-start | bytes 131072 | tf_op jit(solution)/shard_map/psum | solution.py:56
  131.9 291.3 %all-reduce.9.cloned.1.call-start = ((), (), s32[]{:S(2)}) async-start(), calls=%async_computation.2 | async-start | bytes 131072 | tf_op jit(solution)/shard_map/pmax | solution.py:55
  247.5 65.9 %copy-start.4 = (s32[1024]{0:T(1024)S(1)}, s32[1024]{0:T(1024)}, u32[]{:S(2)}) copy-start(s32[1024]{0:T(1024)} %param.18) | copy-start | bytes 12292
  317.5 220.3 %all-reduce.11.cloned.1.call-start = ((), (), s32[]{:S(2)}) async-start(), calls=%async_computation.3 | async-start | bytes 131072 | tf_op jit(solution)/shard_map/psum | solution.py:56
  423.3 114.6 %copy-start.3 = (f32[16384]{0:T(1024)S(1)}, f32[16384]{0:T(1024)}, u32[]{:S(2)}) copy-start(f32[16384]{0:T(1024)} %all-reduce.9.cloned.1.call-done) | copy-start | bytes 196612
  424.8 195.6 %all-gather.6.cloned.1.call-start = ((), (), s32[]{:S(2)}) async-start(), calls=%async_computation.4 | async-start | bytes 4325376 | tf_op jit(solution)/shard_map/all_gather | solution.py:13
  427.6 113.2 %copy-start.2 = (bf16[32,32,256]{2,1,0:T(8,128)(2,1)S(1)}, bf16[32,32,256]{2,1,0:T(8,128)(2,1)}, u32[]{:S(2)}) copy-start(bf16[32,32,256]{2,1,0:T(8,128)(2,1)} %gather_fusion.9) | copy-start | bytes 1572868
Sparse Core Ops, SparseCore 0:
  14.9 115.4 all-reduce.4
  133.9 111.1 all-reduce.6
  317.7 105.5 all-reduce.8
  426.6 111.1 all-reduce.10
  544.7 75.6 all-gather.5
where the time goes:
time: 666 us; the launch traced here: 665 us
  waiting for transfers between devices  455 us (68%)
  blocking collectives  124 us (19%)
  other arithmetic  49.6 us (7%)
  local copies, waits for them, and re-layouts  17.4 us (3%)
  between operations  13.5 us (2%)
    psum x2, waiting for transfers between devices, on_device(): total = lax.psum(local_total * jnp.exp(local_peak - peak), 'state')  223 us
    pmax x2, waiting for transfers between devices, on_device(): peak = lax.pmax(local_peak, 'state')  219 us
    all_gather x4, blocking collectives, combined_all(): pieces = jax.tree.map(lambda part: lax.all_gather(part, axis), value)  124 us
    add x93, other arithmetic, combine_pairs(): a * left + b * right  30.7 us
  transfers between devices with their start and end apart: 5, of which 5 were waited for; matrix products, arithmetic and copies ran while one was open for 1% of the time, Pallas kernels for 0%

commit v1 on v0

v1 whole, which is shorter than its diff:
```python
import jax
import jax.numpy as jnp
from jax import lax
from jax.experimental import pallas as pl
from jax.experimental.pallas import tpu as pltpu
from jax.sharding import PartitionSpec as P

NEG = -1e30
TINY = 1e-30
LANES = 128
UNROLL = 4
F32 = jnp.float32


def vmem(count):
    return [pl.BlockSpec(memory_space=pltpu.VMEM)] * count


def smem(count):
    return [pl.BlockSpec(memory_space=pltpu.SMEM)] * count


def params():
    return pltpu.CompilerParams(vmem_limit_bytes=40 * 1024 * 1024)


def state_beta(temps, betas_ref):
    beta = jnp.zeros(temps.shape, F32)
    for i in range(betas_ref.shape[0]):
        beta = jnp.where(temps == i, betas_ref[i], beta)
    return beta


def expand(rows, cols_ref):
    turned = rows.T
    size = cols_ref.shape[1]
    each = LANES // size
    for j in range(rows.shape[0]):
        wide = jnp.broadcast_to(turned[:, j:j + 1], (LANES, LANES))
        for i in range(each):
            cols_ref[each * j + i] = wide[i * size:(i + 1) * size]
    cols_ref[cols_ref.shape[0] - 1] = jnp.zeros(cols_ref.shape[1:], F32)


def live_groups(cols_ref, blocks):
    live = jnp.int32(0)
    for t in range(cols_ref.shape[0]):
        live = live + (cols_ref[t] < blocks).astype(jnp.int32)
    return (live + UNROLL - 1) // UNROLL


def each_tile(groups, rows_ref, cols_ref, blocks, spare, visit):
    def group(g, carry):
        for i in range(UNROLL):
            t = g * UNROLL + i
            col = cols_ref[t]
            visit(t, jnp.where(col < blocks, rows_ref[t], spare), col)
        return carry

    lax.fori_loop(0, groups, group, 0)


def halves(energies_ref, t):
    count = energies_ref.shape[2] // LANES
    return [energies_ref[t, :, h * LANES:(h + 1) * LANES] for h in range(count)]


def copies(out_ref, value):
    for i in range(out_ref.shape[0]):
        out_ref[i] = value


def first_samples(rows_ref, cols_ref, betas_ref, energies_ref, free_ref, temps_ref, counts_ref, out_ref,
                  beta_cols, bias_cols, peak, total):
    blocks = beta_cols.shape[0] - 1
    blocks_samp = out_ref.shape[1] // peak.shape[0]
    groups = live_groups(cols_ref, blocks)
    expand(state_beta(temps_ref[...], betas_ref), beta_cols)
    expand(jnp.log(counts_ref[...].astype(F32)) + free_ref[...], bias_cols)
    peak[...] = jnp.full(peak.shape, NEG, F32)
    total[...] = jnp.zeros(total.shape, F32)

    def find_peak(t, row, col):
        beta, bias = beta_cols[col], bias_cols[col]
        for h, energy in enumerate(halves(energies_ref, t)):
            top = jnp.max(bias - beta * energy, axis=0, keepdims=True)
            peak[h, pl.ds(row, 1)] = jnp.maximum(peak[h, pl.ds(row, 1)], top)

    def add_up(t, row, col):
        beta, bias = beta_cols[col], bias_cols[col]
        for h, energy in enumerate(halves(energies_ref, t)):
            part = jnp.exp(bias - beta * energy - peak[h, pl.ds(row, 1)])
            total[h, pl.ds(row, 1)] += jnp.sum(part, axis=0, keepdims=True)

    each_tile(groups, rows_ref, cols_ref, blocks, blocks_samp, find_peak)
    each_tile(groups, rows_ref, cols_ref, blocks, blocks_samp, add_up)
    for h in range(peak.shape[0]):
        whole = peak[h, :blocks_samp] + jnp.log(jnp.maximum(total[h, :blocks_samp], 1.0))
        for i in range(out_ref.shape[0]):
            out_ref[i, h * blocks_samp:(h + 1) * blocks_samp] = whole


def load_drop(drop_ref, drop):
    blocks_samp = drop_ref.shape[0] // drop.shape[0]
    for h in range(drop.shape[0]):
        drop[h, :blocks_samp] = drop_ref[h * blocks_samp:(h + 1) * blocks_samp]
        drop[h, blocks_samp:] = jnp.zeros((drop.shape[1] - blocks_samp, LANES), F32)


def first_states(rows_ref, cols_ref, betas_ref, energies_ref, temps_ref, parts_ref, out_ref, drop_ref,
                 beta_cols, drop, top, total):
    blocks = beta_cols.shape[0] - 1
    blocks_samp = drop_ref.shape[0] // drop.shape[0]
    groups = live_groups(cols_ref, blocks)
    expand(state_beta(temps_ref[...], betas_ref), beta_cols)
    peak = jnp.max(parts_ref[...], axis=0)
    whole = jnp.sum(jnp.exp(parts_ref[...] - peak[None]), axis=0)
    drop_ref[...] = peak + jnp.log(jnp.maximum(whole, 1.0))
    load_drop(drop_ref, drop)
    top[...] = jnp.full(top.shape, NEG, F32)
    total[...] = jnp.zeros(total.shape, F32)

    def find_top(t, row, col):
        beta = beta_cols[col]
        for h, energy in enumerate(halves(energies_ref, t)):
            top[col] = jnp.maximum(top[col], -(beta * energy) - drop[h, pl.ds(row, 1)])

    def add_up(t, row, col):
        beta, most = beta_cols[col], top[col]
        part = jnp.zeros(most.shape, F32)
        for h, energy in enumerate(halves(energies_ref, t)):
            part = part + jnp.exp(-(beta * energy) - drop[h, pl.ds(row, 1)] - most)
        total[col] += part

    each_tile(groups, rows_ref, cols_ref, blocks, blocks_samp, find_top)
    for c in range(blocks):
        top[c] = jnp.broadcast_to(jnp.max(top[c], axis=1, keepdims=True), top.shape[1:])
    each_tile(groups, rows_ref, cols_ref, blocks, blocks_samp, add_up)
    each = LANES // top.shape[1]
    lane = lax.broadcasted_iota(jnp.int32, (LANES, LANES), 1)
    turned = jnp.zeros((LANES, LANES), F32)
    for j in range(blocks // each):
        column = [
            top[c] + jnp.log(jnp.maximum(jnp.sum(total[c], axis=1, keepdims=True), 1.0))
            for c in range(each * j, each * j + each)
        ]
        turned = jnp.where(lane == j, jnp.concatenate(column, axis=0), turned)
    copies(out_ref, turned.T[:blocks // each])


def second_samples(rows_ref, cols_ref, betas_ref, energies_ref, temps_ref, counts_ref, drop_ref, parts_ref,
                   out_ref, bias_ref, beta_cols, bias_cols, drop, total):
    blocks = beta_cols.shape[0] - 1
    blocks_samp = drop_ref.shape[0] // drop.shape[0]
    groups = live_groups(cols_ref, blocks)
    top = jnp.max(parts_ref[...], axis=0)
    free = -(top + jnp.log(jnp.sum(jnp.exp(parts_ref[...] - top[None]), axis=0)))
    bias_ref[...] = jnp.log(counts_ref[...].astype(F32)) + free
    expand(state_beta(temps_ref[...], betas_ref), beta_cols)
    expand(bias_ref[...], bias_cols)
    load_drop(drop_ref, drop)
    total[...] = jnp.zeros(total.shape, F32)

    def add_up(t, row, col):
        beta, bias = beta_cols[col], bias_cols[col]
        for h, energy in enumerate(halves(energies_ref, t)):
            part = jnp.exp(bias - beta * energy - drop[h, pl.ds(row, 1)])
            whole = jnp.maximum(jnp.sum(part, axis=0, keepdims=True), jnp.max(part, axis=0, keepdims=True))
            total[h, pl.ds(row, 1)] += whole

    each_tile(groups, rows_ref, cols_ref, blocks, blocks_samp, add_up)
    for h in range(total.shape[0]):
        whole = total[h, :blocks_samp]
        for i in range(out_ref.shape[0]):
            out_ref[i, h * blocks_samp:(h + 1) * blocks_samp] = whole


def second_states(rows_ref, cols_ref, betas_ref, energies_ref, temps_ref, bias_ref, drop_ref, parts_ref, basis_ref,
                  out_ref, beta_cols, bias_cols, drop, values):
    blocks = beta_cols.shape[0] - 1
    blocks_samp = drop_ref.shape[0] // drop.shape[0]
    count = basis_ref.shape[0]
    width = energies_ref.shape[2]
    groups = live_groups(cols_ref, blocks)
    expand(state_beta(temps_ref[...], betas_ref), beta_cols)
    expand(bias_ref[...], bias_cols)
    whole = drop_ref[...] + jnp.log(jnp.maximum(jnp.sum(parts_ref[...], axis=0), TINY))
    for h in range(drop.shape[0]):
        drop[h, :blocks_samp] = whole[h * blocks_samp:(h + 1) * blocks_samp]
        drop[h, blocks_samp:] = jnp.zeros((drop.shape[1] - blocks_samp, LANES), F32)
    values[...] = jnp.zeros(values.shape, F32)
    ones = jnp.ones((values.shape[1] - count, width), jnp.bfloat16)

    def add_up(t, row, col):
        beta, bias = beta_cols[col], bias_cols[col]
        weight = jnp.concatenate(
            [
                jnp.exp(bias - beta * energy - drop[h, pl.ds(row, 1)])
                for h, energy in enumerate(halves(energies_ref, t))
            ],
            axis=1,
        )
        high = weight.astype(jnp.bfloat16)
        low = (weight - high.astype(F32)).astype(jnp.bfloat16)
        start = pl.multiple_of(jnp.minimum(row, blocks_samp - 1) * width, width)
        factor = jnp.concatenate([basis_ref[:, pl.ds(start, width)], ones], axis=0)
        dims = (((1,), (1,)), ((), ()))
        values[col] += lax.dot_general(factor, high, dims, preferred_element_type=F32) + lax.dot_general(
            factor, low, dims, preferred_element_type=F32
        )

    each_tile(groups, rows_ref, cols_ref, blocks, blocks_samp, add_up)
    each = LANES // values.shape[2]
    across = blocks // each
    for j in range(across):
        wide = jnp.concatenate([values[c] for c in range(each * j, each * j + each)], axis=1)
        for g in range(count // 8):
            out_ref[g * across + j, :8] = wide[8 * g:8 * g + 8]
            out_ref[g * across + j, 8:9] = wide[count:count + 1]


def finish(parts_ref, out_ref):
    both = jnp.sum(parts_ref[...], axis=0)
    copies(out_ref, both[:8] / both[8:9])


def spread(parts, axis):
    return lax.all_to_all(parts, axis, 0, 0)


def on_device(n_samp, n_state, energies, tile_rows, tile_cols, start_free, temps, betas, counts, basis):
    slots, state_block, sample_block = energies.shape
    state_dev = start_free.shape[0]
    blocks = state_dev // state_block
    blocks_samp = basis.shape[1] // sample_block
    cut = sample_block // LANES
    rows = state_dev // LANES
    free = start_free.reshape(rows, LANES)
    temps = temps.reshape(rows, LANES)
    counts = counts.reshape(rows, LANES)
    shape = lambda *dims: jax.ShapeDtypeStruct(dims, F32)
    by_state = pltpu.VMEM((blocks + 1, state_block, LANES), F32)
    by_sample = pltpu.VMEM((cut, blocks_samp + 8, LANES), F32)
    parts = pl.pallas_call(
        first_samples,
        out_shape=shape(n_state, cut * blocks_samp, LANES),
        in_specs=smem(3) + vmem(4),
        out_specs=pl.BlockSpec(memory_space=pltpu.VMEM),
        scratch_shapes=[by_state, by_state, by_sample, by_sample],
        compiler_params=params(),
    )(tile_rows, tile_cols, betas, energies, free, temps, counts)
    parts = spread(parts, "state")
    parts, drop = pl.pallas_call(
        first_states,
        out_shape=(shape(n_samp, rows, LANES), shape(cut * blocks_samp, LANES)),
        in_specs=smem(3) + vmem(3),
        out_specs=tuple(vmem(2)),
        scratch_shapes=[by_state, by_sample, by_state, by_state],
        compiler_params=params(),
    )(tile_rows, tile_cols, betas, energies, temps, parts)
    parts = spread(parts, "samp")
    parts, bias = pl.pallas_call(
        second_samples,
        out_shape=(shape(n_state, cut * blocks_samp, LANES), shape(rows, LANES)),
        in_specs=smem(3) + vmem(5),
        out_specs=tuple(vmem(2)),
        scratch_shapes=[by_state, by_state, by_sample, by_sample],
        compiler_params=params(),
    )(tile_rows, tile_cols, betas, energies, temps, counts, drop, parts)
    parts = spread(parts, "state")
    count = basis.shape[0]
    parts = pl.pallas_call(
        second_states,
        out_shape=shape(n_samp, 9, LANES),
        in_specs=smem(3) + vmem(6),
        out_specs=pl.BlockSpec(memory_space=pltpu.VMEM),
        scratch_shapes=[by_state, by_state, by_sample, pltpu.VMEM((blocks + 1, count + 16, state_block), F32)],
        compiler_params=params(),
    )(tile_rows, tile_cols, betas, energies, temps, bias, drop, parts, basis)
    parts = spread(parts, "samp")
    parts = pl.pallas_call(
        finish,
        out_shape=shape(n_samp, 8, LANES),
        in_specs=vmem(1),
        out_specs=pl.BlockSpec(memory_space=pltpu.VMEM),
        compiler_params=params(),
    )(parts)
    parts = spread(parts, "samp")
    return parts.reshape(count // 8, rows, 8, LANES).transpose(0, 2, 1, 3).reshape(count, state_dev)


def solution(mesh):
    n_samp, n_state = mesh.shape["samp"], mesh.shape["state"]

    def run(*args):
        return on_device(n_samp, n_state, *args)

    return jax.shard_map(
        run,
        mesh=mesh,
        in_specs=(
            P(("samp", "state"), None, None),
            P(("samp", "state")),
            P(("samp", "state")),
            P("state"),
            P("state"),
            P(),
            P("state"),
            P(None, "samp"),
        ),
        out_specs=P(None, "state"),
        check_vma=False,
    )
```

time: 666 us -> 137 us (0.21)
  waiting for transfers between devices: 455 us -> 0 us
  other arithmetic: 49.6 us -> 0 us
  between operations: 13.5 us -> 0.05 us
  local copies, waits for them, and re-layouts: 17.4 us -> 6.28 us
    psum x2 -> x0, waiting for transfers between devices: 223 us -> none  [on_device(): total = lax.psum(local_total * jnp.exp(local_peak - peak), 'state')]
    pmax x2 -> x0, waiting for transfers between devices: 219 us -> none  [on_device(): peak = lax.pmax(local_peak, 'state')]
    all_to_all x0 -> x5, blocking collectives: none -> 125 us  [spread(): return lax.all_to_all(parts, axis, 0, 0)]
    all_gather x4 -> x0, blocking collectives: 124 us -> none  [combined_all(): pieces = jax.tree.map(lambda part: lax.all_gather(part, axis), value)]
    add x97 -> x0, other arithmetic: 33.1 us -> none  [the longest x93 30.7 us: combine_pairs(): a * left + b * right]
    all_gather x1 -> x0, waiting for transfers between devices: 12.4 us -> none  [combined_all(): pieces = jax.tree.map(lambda part: lax.all_gather(part, axis), value)]
  transfers between devices with their start and end apart: 5 -> 0, of which waited for: 5 -> 0; matrix products, arithmetic and copies ran while one was open for 1% -> 0% of each run, Pallas kernels for 0% -> 0%
where the time goes in v1:
time: 137 us
  blocking collectives  125 us (91%)
  local copies, waits for them, and re-layouts  6.28 us (5%)
  Pallas kernels  5.66 us (4%)
    all_to_all x5, blocking collectives, spread(): return lax.all_to_all(parts, axis, 0, 0)  125 us
    unnamed x21, local copies, waits for them, and re-layouts  6.28 us

profile of v1, /device:TPU:1, one launch (start us, length us, event | category | flops | bytes accessed | tf_op | source)
XLA Modules:
  0.0 137.0 jit_solution(4908879343906452638)
XLA Ops:
  0.0 0.0 copy-start
  0.0 1.6 %copy-done = f32[32,64,256]{2,1,0:T(8,128)S(1)} copy-done((f32[32,64,256]{2,1,0:T(8,128)S(1)}, f32[32,64,256]{2,1,0:T(8,128)}, u32[]{:S(2)}) %copy-start) | copy-done | bytes 2097176
  1.6 0.0 copy-start.2
  1.6 0.7 copy-done.2
  2.3 0.0 copy-start.4
  2.3 0.7 copy-done.4
  3.0 0.0 copy-start.6
  3.0 0.7 copy-done.6
  3.6 0.0 copy-start.7
  3.6 0.7 copy-done.7
  4.3 0.0 copy-start.8
  4.3 0.7 copy-done.8
  4.9 0.0 copy-start.9
  4.9 0.7 copy-done.9
  5.6 0.0 copy-start.3
  5.6 1.2 shard_map.82
  6.9 22.4 %all_to_all.25.parts_ref = f32[16,128,128]{2,1,0:T(8,128)S(1)} all-to-all(f32[16,128,128]{2,1,0:T(8,128)S(1)} %shard_map.82), channel_id=1, replica_groups=mesh['samp'=32,'state'=16] {'state'}, dimensions={0} | all-to-all | bytes 2097152 | tf_op jit(solution)/shard_map/all_to_all | solution.py:228
  29.3 0.0 copy-done.3
  29.3 0.0 copy-start.5
  29.3 1.7 %shard_map.83 = (f32[32,8,128]{2,1,0:T(8,128)S(1)}, f32[128,128]{1,0:T(8,128)S(1)}) custom-call(s32[32]{0:T(128)S(1)} %copy-done.6, s32[32]{0:T(128)S(1)} %copy-done.7, f32[16]{0:T(128)S(1)} %copy-done.8, f32[32,64,256]{2,1,0:T(8,128)S(1)} %copy-done, s32[8,128]{1,0:T(8,128)S(1)} %bitcast.9, f32[16,128,128]{2,1,0:T(8,128)S(1)} %all_to_all.25.parts_ref), custom_call_target="tpu_custom_call" | custom-call | tf_op jit(solution)/shard_map/pallas_call | solution.py:253
  31.0 34.5 %all_to_all.26.parts_ref = f32[32,8,128]{2,1,0:T(8,128)S(1)} all-to-all(f32[32,8,128]{2,1,0:T(8,128)S(1)} %get-tuple-element.10), channel_id=1, replica_groups=mesh['samp'=32,'state'=16] {'samp'}, dimensions={0} | all-to-all | bytes 262144 | tf_op jit(solution)/shard_map/all_to_all | solution.py:228
  65.4 0.0 copy-done.5
  65.4 0.0 copy-start.1
  65.4 1.3 shard_map.84
  66.8 18.1 %all_to_all.27.parts_ref = f32[16,128,128]{2,1,0:T(8,128)S(1)} all-to-all(f32[16,128,128]{2,1,0:T(8,128)S(1)} %get-tuple-element.12), channel_id=1, replica_groups=mesh['samp'=32,'state'=16] {'state'}, dimensions={0} | all-to-all | bytes 2097152 | tf_op jit(solution)/shard_map/all_to_all | solution.py:228
  84.8 0.0 copy-done.1
  84.8 1.4 shard_map.85
  86.2 30.3 %all_to_all.28.parts_ref = f32[32,9,128]{2,1,0:T(8,128)S(1)} all-to-all(f32[32,9,128]{2,1,0:T(8,128)S(1)} %shard_map.85), channel_id=1, replica_groups=mesh['samp'=32,'state'=16] {'samp'}, dimensions={0} | all-to-all | bytes 294912 | tf_op jit(solution)/shard_map/all_to_all | solution.py:228
  116.6 19.8 %all_to_all.29 = f32[32,8,128]{2,1,0:T(8,128)S(1)} all-to-all(f32[32,8,128]{2,1,0:T(8,128)S(1)} %shard_map.86), channel_id=1, replica_groups=mesh['samp'=32,'state'=16] {'samp'}, dimensions={0} | all-to-all | bytes 262144 | tf_op jit(solution)/shard_map/all_to_all | solution.py:228
  136.4 0.7 copy.10
  (1 shorter events, 0.0 us)
Async XLA Ops:
  0.0 1.6 %copy-start = (f32[32,64,256]{2,1,0:T(8,128)S(1)}, f32[32,64,256]{2,1,0:T(8,128)}, u32[]{:S(2)}) copy-start(f32[32,64,256]{2,1,0:T(8,128)} %energies_ref.7) | copy-start | bytes 6291460
  1.6 0.7 copy-start.2
  2.3 0.7 copy-start.4
  3.0 0.7 copy-start.6
  3.6 0.7 copy-start.7
  4.3 0.7 copy-start.8
  4.9 0.7 copy-start.9
  5.6 23.6 %copy-start.3 = (s32[1024]{0:T(1024)S(1)}, s32[1024]{0:T(1024)}, u32[]{:S(2)}) copy-start(s32[1024]{0:T(1024)} %param.12) | copy-start | bytes 12292
  29.3 36.2 %copy-start.5 = (s32[1024]{0:T(1024)S(1)}, s32[1024]{0:T(1024)}, u32[]{:S(2)}) copy-start(s32[1024]{0:T(1024)} %param.14) | copy-start | bytes 12292
  65.4 19.4 %copy-start.1 = (bf16[32,16384]{1,0:T(8,128)(2,1)S(1)}, bf16[32,16384]{1,0:T(8,128)(2,1)}, u32[]{:S(2)}) copy-start(bf16[32,16384]{1,0:T(8,128)(2,1)} %basis_ref.1) | copy-start | bytes 3145732

commit v2 on v1

v2 whole, which is shorter than its diff:
```python
import jax
import jax.numpy as jnp
from jax import lax
from jax.experimental import pallas as pl
from jax.experimental.pallas import tpu as pltpu
from jax.sharding import Mesh, PartitionSpec as P

NEG = -1e30
TINY = 1e-30
LANES = 128
UNROLL = 4
F32 = jnp.float32
BF16 = jnp.bfloat16
STEP = 64.0
BASE = -256.0
LAST = 11.0
BITS = 10.0


def vmem(count):
    return [pl.BlockSpec(memory_space=pltpu.VMEM)] * count


def smem(count):
    return [pl.BlockSpec(memory_space=pltpu.SMEM)] * count


def hbm(count):
    return [pl.BlockSpec(memory_space=pltpu.HBM)] * count


def params():
    return pltpu.CompilerParams(vmem_limit_bytes=40 * 1024 * 1024)


def expand(rows, cols_ref):
    turned = rows.T
    size = cols_ref.shape[1]
    each = LANES // size
    for j in range(rows.shape[0]):
        wide = jnp.broadcast_to(turned[:, j:j + 1], (LANES, LANES))
        for i in range(each):
            cols_ref[each * j + i] = wide[i * size:(i + 1) * size]
    cols_ref[cols_ref.shape[0] - 1] = jnp.zeros(cols_ref.shape[1:], F32)


def count_live(cols_ref, blocks):
    live = jnp.int32(0)
    for t in range(cols_ref.shape[0]):
        live = live + (cols_ref[t] < blocks).astype(jnp.int32)
    return live


def each_tile(live, rows_ref, cols_ref, spare, visit):
    def group(g, carry):
        for i in range(UNROLL):
            t = g * UNROLL + i
            visit(t, jnp.where(t < live, rows_ref[t], spare), cols_ref[t])
        return carry

    lax.fori_loop(0, (live + UNROLL - 1) // UNROLL, group, 0)


def halves(energies_ref, t):
    count = energies_ref.shape[2] // LANES
    return [energies_ref[t, :, h * LANES:(h + 1) * LANES] for h in range(count)]


def copies(out_ref, value):
    for i in range(out_ref.shape[0]):
        out_ref[i] = value


def log_sum(parts):
    top = jnp.max(parts, axis=0)
    return top + jnp.log(jnp.sum(jnp.exp(parts - top[None]), axis=0))


def row_sums(hot, values):
    total = None
    for _ in range(3):
        part = values.astype(BF16)
        values = values - part.astype(F32)
        product = jnp.dot(hot, part, preferred_element_type=F32)
        total = product if total is None else total + product
    return total


def by_half(parts_ref, half, slots):
    values = parts_ref[:, half * slots:(half + 1) * slots]
    return values.reshape(values.shape[0] * slots, LANES)


def first_samples(rows_hbm, cols_hbm, betas_hbm, energies_hbm, free_hbm, temps_hbm, counts_hbm,
                  out_ref, beta_ref, count_ref,
                  rows_ref, cols_ref, betas_ref, energies_ref, free_ref, temps_ref, counts_ref,
                  beta_cols, bias_cols, slot, sems):
    blocks = beta_cols.shape[0] - 1
    slots = energies_ref.shape[0]
    cut = energies_ref.shape[2] // LANES
    small = [
        pltpu.make_async_copy(source, target, sems.at[i])
        for i, (source, target) in enumerate([
            (temps_hbm, temps_ref), (counts_hbm, counts_ref), (free_hbm, free_ref),
            (betas_hbm, betas_ref), (cols_hbm, cols_ref), (rows_hbm, rows_ref),
        ])
    ]
    large = [
        pltpu.make_async_copy(
            energies_hbm.at[pl.ds(g * UNROLL, UNROLL)], energies_ref.at[pl.ds(g * UNROLL, UNROLL)],
            sems.at[len(small) + g],
        )
        for g in range(slots // UNROLL)
    ]
    for copy in small + large:
        copy.start()
    for copy in small:
        copy.wait()
    temps = temps_ref[...]
    beta = jnp.zeros(temps.shape, F32)
    for i in range(betas_ref.shape[0]):
        beta = jnp.where(temps == i, betas_ref[i], beta)
    beta_ref[...] = beta
    count_ref[...] = jnp.log(counts_ref[...].astype(F32))
    expand(beta, beta_cols)
    expand(count_ref[...] + free_ref[...], bias_cols)
    live = count_live(cols_ref, blocks)
    slot[...] = jnp.full(slot.shape, NEG, F32)
    lane = lax.broadcasted_iota(jnp.int32, (1, LANES), 1)
    places = jnp.zeros((1, LANES), F32)
    for t in range(slots):
        places = jnp.where(lane == t, rows_ref[t].astype(F32), places)
    slot[cut * slots:cut * slots + 1] = places
    for g in range(slots // UNROLL):
        large[g].wait()

        @pl.when(g * UNROLL < live)
        def _():
            for t in range(g * UNROLL, (g + 1) * UNROLL):
                beta, bias = beta_cols[cols_ref[t]], bias_cols[cols_ref[t]]
                for h, energy in enumerate(halves(energies_ref, t)):
                    score = bias - beta * energy
                    peak = jnp.max(score, axis=0, keepdims=True)
                    total = jnp.sum(jnp.exp(score - peak), axis=0, keepdims=True)
                    whole = peak + jnp.log(jnp.maximum(total, 1.0))
                    slot[h * slots + t:h * slots + t + 1] = jnp.where(t < live, whole, NEG)

    copies(out_ref, slot[...])


def load_drop(value, drop):
    blocks_samp = value.shape[0] // drop.shape[0]
    for h in range(drop.shape[0]):
        drop[h, :blocks_samp] = value[h * blocks_samp:(h + 1) * blocks_samp]
        drop[h, blocks_samp:] = jnp.zeros((drop.shape[1] - blocks_samp, LANES), F32)


def first_states(rows_ref, cols_ref, energies_ref, beta_ref, parts_ref, out_ref, drop_ref, hot_ref,
                 beta_cols, drop, top, total):
    blocks = beta_cols.shape[0] - 1
    cut = drop.shape[0]
    blocks_samp = drop_ref.shape[0] // cut
    slots = energies_ref.shape[0]
    live = count_live(cols_ref, blocks)
    expand(beta_ref[...], beta_cols)
    wide = []
    for j in range(parts_ref.shape[0] * slots // LANES):
        places = jnp.zeros((1, LANES), F32)
        for i in range(LANES // slots):
            place = parts_ref[j * (LANES // slots) + i, cut * slots:cut * slots + 1]
            places = places + (pltpu.roll(place, i * slots, 1) if i else place)
        wide.append(places)
    wide = jnp.concatenate(wide, axis=1)
    row = lax.broadcasted_iota(jnp.int32, (blocks_samp, wide.shape[1]), 0).astype(F32)
    hot = jnp.where(row == wide, 1.0, 0.0).astype(BF16)
    hot_ref[...] = hot
    parts = jnp.concatenate([by_half(parts_ref, h, slots) for h in range(cut)], axis=1)
    step = jnp.clip(jnp.floor((parts - BASE) * (1.0 / STEP)), 0.0, LAST)
    power = jnp.exp2(BITS * step).astype(BF16)
    found = jnp.maximum(jnp.dot(hot, power, preferred_element_type=F32), 1.0)
    step = jnp.floor(jnp.log2(found) * (1.0 / BITS) + 0.03)
    back = lax.dot_general(hot, step.astype(BF16), (((0,), (0,)), ((), ())), preferred_element_type=F32)
    whole = row_sums(hot, jnp.exp(parts - (BASE + STEP * back)))
    whole = BASE + STEP * step + jnp.log(jnp.maximum(whole, 0.5))
    for h in range(cut):
        drop_ref[h * blocks_samp:(h + 1) * blocks_samp] = whole[:, h * LANES:(h + 1) * LANES]
    load_drop(drop_ref[...], drop)
    top[...] = jnp.full(top.shape, NEG, F32)
    total[...] = jnp.zeros(total.shape, F32)

    def find_top(t, row, col):
        beta = beta_cols[col]
        for h, energy in enumerate(halves(energies_ref, t)):
            top[col] = jnp.maximum(top[col], -(beta * energy) - drop[h, pl.ds(row, 1)])

    def add_up(t, row, col):
        beta, most = beta_cols[col], top[col]
        part = jnp.zeros(most.shape, F32)
        for h, energy in enumerate(halves(energies_ref, t)):
            part = part + jnp.exp(-(beta * energy) - drop[h, pl.ds(row, 1)] - most)
        total[col] += part

    each_tile(live, rows_ref, cols_ref, blocks_samp, find_top)
    for c in range(blocks):
        top[c] = jnp.broadcast_to(jnp.max(top[c], axis=1, keepdims=True), top.shape[1:])
    each_tile(live, rows_ref, cols_ref, blocks_samp, add_up)
    each = LANES // top.shape[1]
    lane = lax.broadcasted_iota(jnp.int32, (LANES, LANES), 1)
    turned = jnp.zeros((LANES, LANES), F32)
    for j in range(blocks // each):
        column = [
            top[c] + jnp.log(jnp.maximum(jnp.sum(total[c], axis=1, keepdims=True), 1.0))
            for c in range(each * j, each * j + each)
        ]
        turned = jnp.where(lane == j, jnp.concatenate(column, axis=0), turned)
    out_ref[...] = turned.T[:blocks // each]


def both_cores(parts_ref, out_ref):
    copies(out_ref, log_sum(parts_ref[...]))


def second_samples(rows_ref, cols_ref, energies_ref, beta_ref, count_ref, drop_ref, parts_ref,
                   out_ref, bias_ref, beta_cols, bias_cols, drop, slot):
    blocks = beta_cols.shape[0] - 1
    cut = drop.shape[0]
    blocks_samp = drop_ref.shape[0] // cut
    slots = energies_ref.shape[0]
    live = count_live(cols_ref, blocks)
    bias_ref[...] = count_ref[...] - log_sum(parts_ref[...])
    expand(beta_ref[...], beta_cols)
    expand(bias_ref[...], bias_cols)
    load_drop(drop_ref[...], drop)
    slot[...] = jnp.zeros(slot.shape, F32)
    for g in range(slots // UNROLL):

        @pl.when(g * UNROLL < live)
        def _():
            for t in range(g * UNROLL, (g + 1) * UNROLL):
                beta, bias = beta_cols[cols_ref[t]], bias_cols[cols_ref[t]]
                for h, energy in enumerate(halves(energies_ref, t)):
                    part = jnp.exp(bias - beta * energy - drop[h, pl.ds(rows_ref[t], 1)])
                    whole = jnp.maximum(jnp.sum(part, axis=0, keepdims=True), jnp.max(part, axis=0, keepdims=True))
                    slot[h * slots + t:h * slots + t + 1] = jnp.where(t < live, whole, 0.0)

    copies(out_ref, slot[...])


def second_states(rows_ref, cols_ref, energies_ref, beta_ref, bias_ref, drop_ref, hot_ref, parts_ref, basis_ref,
                  out_ref, beta_cols, bias_cols, drop, values):
    blocks = beta_cols.shape[0] - 1
    cut = drop.shape[0]
    blocks_samp = drop_ref.shape[0] // cut
    slots = energies_ref.shape[0]
    count = basis_ref.shape[0]
    width = energies_ref.shape[2]
    live = count_live(cols_ref, blocks)
    expand(beta_ref[...], beta_cols)
    expand(bias_ref[...], bias_cols)
    parts = jnp.concatenate([by_half(parts_ref, h, slots) for h in range(cut)], axis=1)
    whole = jnp.log(jnp.maximum(row_sums(hot_ref[...], parts), TINY))
    whole = jnp.concatenate([whole[:, h * LANES:(h + 1) * LANES] for h in range(cut)], axis=0)
    load_drop(drop_ref[...] + whole, drop)
    values[...] = jnp.zeros(values.shape, F32)
    ones = jnp.ones((values.shape[1] - count, width), BF16)

    def add_up(t, row, col):
        beta, bias = beta_cols[col], bias_cols[col]
        weight = jnp.concatenate(
            [
                jnp.exp(bias - beta * energy - drop[h, pl.ds(row, 1)])
                for h, energy in enumerate(halves(energies_ref, t))
            ],
            axis=1,
        )
        high = weight.astype(BF16)
        low = (weight - high.astype(F32)).astype(BF16)
        start = pl.multiple_of(jnp.minimum(row, blocks_samp - 1) * width, width)
        factor = jnp.concatenate([basis_ref[:, pl.ds(start, width)], ones], axis=0)
        dims = (((1,), (1,)), ((), ()))
        values[col] += lax.dot_general(factor, high, dims, preferred_element_type=F32) + lax.dot_general(
            factor, low, dims, preferred_element_type=F32
        )

    each_tile(live, rows_ref, cols_ref, blocks_samp, add_up)
    each = LANES // values.shape[2]
    across = blocks // each
    half = out_ref.shape[1]
    for j in range(across):
        wide = jnp.concatenate([values[c] for c in range(each * j, each * j + each)], axis=1)
        for g in range(count // 8):
            owner = g * across + j
            for r in range(8):
                out_ref[owner // half, owner % half, r] = wide[8 * g + r:8 * g + r + 1]
            out_ref[owner // half, owner % half, 8] = wide[count:count + 1]


def core_sums(parts_ref, out_ref):
    mine = lax.axis_index("core")
    out_ref[...] = parts_ref[0, mine] + parts_ref[1, mine]


def finish(parts_ref, out_ref):
    both = jnp.sum(parts_ref[...], axis=0)
    value = jnp.concatenate([both[r] for r in range(8)], axis=0)
    copies(out_ref, value / both[8])


def spread(parts, axis):
    return lax.all_to_all(parts, axis, 0, 0)


def call(kernel, out_shape, in_specs, scratch_shapes=()):
    single = not isinstance(out_shape, tuple)
    return pl.pallas_call(
        kernel,
        out_shape=out_shape,
        in_specs=in_specs,
        out_specs=vmem(1)[0] if single else tuple(vmem(len(out_shape))),
        scratch_shapes=list(scratch_shapes),
        compiler_params=params(),
    )


def on_device(n_core, n_z, n_state, energies, tile_rows, tile_cols, start_free, temps, betas, counts, basis):
    slots, state_block, sample_block = energies.shape
    state_dev = start_free.shape[0]
    blocks = state_dev // state_block
    blocks_samp = basis.shape[1] // sample_block
    cut = sample_block // LANES
    rows = state_dev // LANES
    count = basis.shape[0]
    shape = lambda *dims: jax.ShapeDtypeStruct(dims, F32)
    by_state = pltpu.VMEM((blocks + 1, state_block, LANES), F32)
    by_sample = pltpu.VMEM((cut, blocks_samp + 8, LANES), F32)
    flat = pltpu.VMEM((rows, LANES), F32)
    whole = pltpu.VMEM((rows, LANES), jnp.int32)

    parts, beta, log_count = call(
        first_samples,
        (shape(n_state, cut * slots + 8, LANES), shape(rows, LANES), shape(rows, LANES)),
        hbm(7),
        [
            pltpu.SMEM(tile_rows.shape, jnp.int32),
            pltpu.SMEM(tile_cols.shape, jnp.int32),
            pltpu.SMEM(betas.shape, F32),
            pltpu.VMEM(energies.shape, F32),
            flat, whole, whole, by_state, by_state,
            pltpu.VMEM((cut * slots + 8, LANES), F32),
            pltpu.SemaphoreType.DMA((6 + slots // UNROLL,)),
        ],
    )(
        tile_rows, tile_cols, betas, energies,
        start_free.reshape(rows, LANES), temps.reshape(rows, LANES), counts.reshape(rows, LANES),
    )
    parts = spread(parts, "state")
    parts, drop, hot = call(
        first_states,
        (
            shape(rows, LANES), shape(cut * blocks_samp, LANES),
            jax.ShapeDtypeStruct((blocks_samp, n_state * slots), BF16),
        ),
        smem(2) + vmem(3),
        [by_state, by_sample, by_state, by_state],
    )(tile_rows, tile_cols, energies, beta, parts)
    parts = lax.all_gather(parts, "core")
    parts = call(both_cores, shape(n_z, rows, LANES), vmem(1))(parts)
    parts = spread(parts, "z")
    parts, bias = call(
        second_samples,
        (shape(n_state, cut * slots, LANES), shape(rows, LANES)),
        smem(2) + vmem(5),
        [by_state, by_state, by_sample, pltpu.VMEM((cut * slots, LANES), F32)],
    )(tile_rows, tile_cols, energies, beta, log_count, drop, parts)
    parts = spread(parts, "state")
    parts = call(
        second_states,
        shape(n_core, n_z, 9, 1, LANES),
        smem(2) + vmem(7),
        [by_state, by_state, by_sample, pltpu.VMEM((blocks + 1, count + 16, state_block), F32)],
    )(tile_rows, tile_cols, energies, beta, bias, drop, hot, parts, basis)
    parts = lax.all_gather(parts, "core")
    parts = call(core_sums, shape(n_z, 9, 1, LANES), vmem(1))(parts)
    parts = spread(parts, "z")
    parts = call(finish, shape(n_z, 8, LANES), vmem(1))(parts)
    parts = spread(parts, "z")
    parts = lax.all_gather(parts, "core")
    return parts.reshape(count // 8, rows, 8, LANES).transpose(0, 2, 1, 3).reshape(count, state_dev)


def solution(mesh):
    n_samp, n_state = mesh.shape["samp"], mesh.shape["state"]
    n_core = 2
    n_z = n_samp // n_core
    cut = Mesh(mesh.devices.reshape(n_z, n_core, n_state), ("z", "core", "state"))
    samp = ("z", "core")

    def run(*args):
        return on_device(n_core, n_z, n_state, *args)

    return jax.shard_map(
        run,
        mesh=cut,
        in_specs=(
            P(("z", "core", "state"), None, None),
            P(("z", "core", "state")),
            P(("z", "core", "state")),
            P("state"),
            P("state"),
            P(),
            P("state"),
            P(None, samp),
        ),
        out_specs=P(None, "state"),
        check_vma=False,
    )
```

time: 137 us -> 116 us (0.85)
  blocking collectives: 125 us -> 101 us
  Pallas kernels: 5.66 us -> 7.67 us
    all_to_all x5, blocking collectives: 125 us -> 88.7 us  [spread(): return lax.all_to_all(parts, axis, 0, 0)]
    all_gather x0 -> x3, blocking collectives: none -> 11.9 us  [on_device(): parts = lax.all_gather(parts, 'core')]
    pallas_call x5 -> x7, Pallas kernels: 5.66 us -> 7.67 us  [the longest x1 2.39 us: on_device(): call(first_states, (shape(rows, LANES), shape(cut * blocks_samp, LANES),...]
    unnamed x21 -> x23, local copies, waits for them, and re-layouts: 6.28 us -> 6.29 us
where the time goes in v2:
time: 116 us; the launch traced here: 115 us
  blocking collectives  101 us (87%)
  Pallas kernels  7.67 us (7%)
  local copies, waits for them, and re-layouts  6.6 us (6%)
    all_to_all x5, blocking collectives, spread(): return lax.all_to_all(parts, axis, 0, 0)  88.7 us
    all_gather x3, blocking collectives, on_device(): parts = lax.all_gather(parts, 'core')  11.9 us
    unnamed x23, local copies, waits for them, and re-layouts  6.29 us
    pallas_call x1, Pallas kernels, on_device(): call(first_states, (shape(rows, LANES), shape(cut * blocks_samp, LANES),...  2.39 us

profile of v2, /device:TPU:1, one launch (start us, length us, event | category | flops | bytes accessed | tf_op | source)
XLA Modules:
  0.0 115.0 jit_solution(14777217702555294080)
XLA Ops:
  0.0 0.0 copy-start
  0.0 1.6 %copy-done = f32[32,64,256]{2,1,0:T(8,128)S(1)} copy-done((f32[32,64,256]{2,1,0:T(8,128)S(1)}, f32[32,64,256]{2,1,0:T(8,128)}, u32[]{:S(2)}) %copy-start) | copy-done | bytes 2097176
  1.6 0.0 copy-start.3
  1.6 0.7 copy-done.3
  2.2 0.0 copy-start.5
  2.2 0.7 copy-done.5
  2.9 0.0 copy-start.7
  2.9 0.7 copy-done.7
  3.6 0.0 copy-start.8
  3.6 0.7 copy-done.8
  4.3 0.0 copy-start.9
  4.3 0.7 copy-done.9
  5.0 0.0 copy-start.10
  5.0 0.7 copy-done.10
  5.6 0.0 copy-start.1
  5.6 1.6 %shard_map.82 = (f32[16,72,128]{2,1,0:T(8,128)S(1)}, f32[8,128]{1,0:T(8,128)S(1)}, f32[8,128]{1,0:T(8,128)S(1)}) custom-call(s32[32]{0:T(128)S(1)} %copy-done.3, s32[32]{0:T(128)S(1)} %copy-done.5, f32[16]{0:T(128)S(1)} %copy-done.10, f32[32,64,256]{2,1,0:T(8,128)S(1)} %copy-done, f32[8,128]{1,0:T(8,128)S(1)} %bitcast.12, s32[8,128]{1,0:T(8,128)S(1)} %bitcast.13, ...), custom_call_target="tpu_custom_call" | custom-call | tf_op jit(solution)/shard_map/pallas_call | solution.py:339
  7.3 0.0 copy-start.4
  7.3 0.0 copy-start.6
  7.3 18.4 %all_to_all.25.parts_ref = f32[16,72,128]{2,1,0:T(8,128)S(1)} all-to-all(f32[16,72,128]{2,1,0:T(8,128)S(1)} %get-tuple-element.15), channel_id=1, replica_groups=mesh['z'=16,'core'=2,'state'=16] {'state'}, dimensions={0} | all-to-all | bytes 1179648 | tf_op jit(solution)/shard_map/all_to_all | solution.py:310
  25.7 0.0 copy-done.1
  25.7 2.4 %shard_map.83 = (f32[8,128]{1,0:T(8,128)S(1)}, f32[128,128]{1,0:T(8,128)S(1)}, bf16[64,512]{1,0:T(8,128)(2,1)S(1)}) custom-call(s32[32]{0:T(128)S(1)} %copy-done.3, s32[32]{0:T(128)S(1)} %copy-done.5, f32[32,64,256]{2,1,0:T(8,128)S(1)} %copy-done.1, f32[8,128]{1,0:T(8,128)S(1)} %get-tuple-element.13.beta_ref, f32[16,72,128]{2,1,0:T(8,128)S(1)} %all_to_all.25.parts_ref), custom_call_target="tpu_custom_call" | custom-call | tf_op jit(solution)/shard_map/pallas_call | solution.py:357
  28.1 0.0 copy-start.2
  28.1 3.8 %all-gather = f32[16,128]{1,0:T(8,128)S(1)} all-gather(f32[8,128]{1,0:T(8,128)S(1)} %get-tuple-element.17), channel_id=2, replica_groups=mesh['z'=16,'core'=2,'state'=16] {'core'}, dimensions={0}, use_global_device_ids=true | all-gather | bytes 12288 | tf_op jit(solution)/shard_map/all_gather | solution.py:366
  31.9 26.5 %all_to_all.26.parts_ref = f32[16,8,128]{2,1,0:T(8,128)S(1)} all-to-all(f32[16,8,128]{2,1,0:T(8,128)S(1)} %shard_map.84), channel_id=1, replica_groups=mesh['z'=16,'core'=2,'state'=16] {'z'}, dimensions={0} | all-to-all | bytes 131072 | tf_op jit(solution)/shard_map/all_to_all | solution.py:310
  58.4 0.0 copy-done.4
  58.4 0.0 copy-done.6
  58.4 1.5 %shard_map.85 = (f32[16,64,128]{2,1,0:T(8,128)S(1)}, f32[8,128]{1,0:T(8,128)S(1)}) custom-call(s32[32]{0:T(128)S(1)} %copy-done.4, s32[32]{0:T(128)S(1)} %copy-done.6, f32[32,64,256]{2,1,0:T(8,128)S(1)} %copy-done.1, f32[8,128]{1,0:T(8,128)S(1)} %get-tuple-element.13.beta_ref, f32[8,128]{1,0:T(8,128)S(1)} %get-tuple-element.14.count_ref, ...), custom_call_target="tpu_custom_call" | custom-call | tf_op jit(solution)/shard_map/pallas_call | solution.py:369
  59.9 12.4 %all_to_all.27.parts_ref = f32[16,64,128]{2,1,0:T(8,128)S(1)} all-to-all(f32[16,64,128]{2,1,0:T(8,128)S(1)} %get-tuple-element.20), channel_id=1, replica_groups=mesh['z'=16,'core'=2,'state'=16] {'state'}, dimensions={0} | all-to-all | bytes 1048576 | tf_op jit(solution)/shard_map/all_to_all | solution.py:310
  72.3 0.0 copy-done.2
  72.3 2.0 %shard_map.86 = f32[2,16,9,1,128]{4,3,2,1,0:T(1,128)S(1)} custom-call(s32[32]{0:T(128)S(1)} %copy-done.4, s32[32]{0:T(128)S(1)} %copy-done.6, f32[32,64,256]{2,1,0:T(8,128)S(1)} %copy-done.1, f32[8,128]{1,0:T(8,128)S(1)} %get-tuple-element.13.beta_ref, f32[8,128]{1,0:T(8,128)S(1)} %get-tuple-element.18.bias_ref, f32[128,128]{1,0:T(8,128)S(1)} %get-tuple-element.16.drop_ref, ...), custom_call_target="tpu_custom_call" | custom-call | tf_op jit(solution)/shard_map/pallas_call | solution.py:376
  74.4 4.2 %all-gather.1 = f32[4,16,9,1,128]{4,1,3,2,0:T(8,128)S(1)} all-gather(f32[2,16,9,1,128]{4,1,3,2,0:T(8,128)S(1)} %copy.9), channel_id=3, replica_groups=mesh['z'=16,'core'=2,'state'=16] {'core'}, dimensions={0}, use_global_device_ids=true | all-gather | bytes 442368 | tf_op jit(solution)/shard_map/all_gather | solution.py:382
  78.6 0.3 copy.10
  78.9 0.1 shard_map.87
  79.0 16.0 %all_to_all.28.parts_ref = f32[16,9,1,128]{3,2,1,0:T(1,128)S(1)} all-to-all(f32[16,9,1,128]{3,2,1,0:T(1,128)S(1)} %shard_map.87), channel_id=1, replica_groups=mesh['z'=16,'core'=2,'state'=16] {'z'}, dimensions={0} | all-to-all | bytes 147456 | tf_op jit(solution)/shard_map/all_to_all | solution.py:310
  95.0 0.1 shard_map.88
  95.0 15.4 %all_to_all.29 = f32[16,8,128]{2,1,0:T(8,128)S(1)} all-to-all(f32[16,8,128]{2,1,0:T(8,128)S(1)} %shard_map.88), channel_id=1, replica_groups=mesh['z'=16,'core'=2,'state'=16] {'z'}, dimensions={0} | all-to-all | bytes 131072 | tf_op jit(solution)/shard_map/all_to_all | solution.py:310
  110.4 4.0 %all-gather.2 = f32[32,8,128]{2,1,0:T(8,128)S(1)} all-gather(f32[16,8,128]{2,1,0:T(8,128)S(1)} %all_to_all.29), channel_id=4, replica_groups=mesh['z'=16,'core'=2,'state'=16] {'core'}, dimensions={0}, use_global_device_ids=true | all-gather | bytes 196608 | tf_op jit(solution)/shard_map/all_gather | solution.py:387
  114.4 0.7 copy.12
  (2 shorter events, 0.0 us)
Async XLA Ops:
  0.0 1.6 %copy-start = (f32[32,64,256]{2,1,0:T(8,128)S(1)}, f32[32,64,256]{2,1,0:T(8,128)}, u32[]{:S(2)}) copy-start(f32[32,64,256]{2,1,0:T(8,128)} %energies_ref.5) | copy-start | bytes 6291460
  1.6 0.7 copy-start.3
  2.2 0.7 copy-start.5
  2.9 0.7 copy-start.7
  3.6 0.7 copy-start.8
  4.3 0.7 copy-start.9
  5.0 0.7 copy-start.10
  5.6 20.1 %copy-start.1 = (f32[32,64,256]{2,1,0:T(8,128)S(1)}, f32[32,64,256]{2,1,0:T(8,128)}, u32[]{:S(2)}) copy-start(f32[32,64,256]{2,1,0:T(8,128)} %energies_ref.5) | copy-start | bytes 6291460
  7.3 51.2 %copy-start.4 = (s32[32]{0:T(128)S(1)}, s32[32]{0:T(128)}, u32[]{:S(2)}) copy-start(s32[32]{0:T(128)} %rows_ref.5) | copy-start | bytes 388
  7.3 51.2 %copy-start.6 = (s32[32]{0:T(128)S(1)}, s32[32]{0:T(128)}, u32[]{:S(2)}) copy-start(s32[32]{0:T(128)} %cols_ref.5) | copy-start | bytes 388
  28.1 44.2 %copy-start.2 = (bf16[32,16384]{1,0:T(8,128)(2,1)S(1)}, bf16[32,16384]{1,0:T(8,128)(2,1)}, u32[]{:S(2)}) copy-start(bf16[32,16384]{1,0:T(8,128)(2,1)} %basis_ref.1) | copy-start | bytes 3145732

commit v3 on v2

v3 whole, which is shorter than its diff:
```python
import jax
import jax.numpy as jnp
from jax import lax
from jax.experimental import pallas as pl
from jax.experimental.pallas import tpu as pltpu
from jax.sharding import Mesh, PartitionSpec as P

NEG = -1e30
TINY = 1e-30
LANES = 128
UNROLL = 4
MIB = 1024 * 1024
FIRST_VMEM = 60 * MIB
F32 = jnp.float32
BF16 = jnp.bfloat16
LOG2E = 1.4426950408889634
STEP = 96.0
BASE = -400.0
LAST = 11.0
BITS = 10.0


def vmem(count):
    return [pl.BlockSpec(memory_space=pltpu.VMEM)] * count


def smem(count):
    return [pl.BlockSpec(memory_space=pltpu.SMEM)] * count


def hbm(count):
    return [pl.BlockSpec(memory_space=pltpu.HBM)] * count


def anywhere(count):
    return [pl.BlockSpec(memory_space=pl.ANY)] * count


def expand(rows, cols_ref, spare):
    turned = rows.T
    size = cols_ref.shape[1]
    each = LANES // size
    for j in range(rows.shape[0]):
        wide = jnp.broadcast_to(turned[:, j:j + 1], (LANES, LANES))
        for i in range(each):
            cols_ref[each * j + i] = wide[i * size:(i + 1) * size]
    cols_ref[cols_ref.shape[0] - 1] = jnp.full(cols_ref.shape[1:], spare, F32)


def halves(energies_ref, t):
    count = energies_ref.shape[2] // LANES
    return [energies_ref[t, :, h * LANES:(h + 1) * LANES] for h in range(count)]


def copies(out_ref, value):
    for i in range(out_ref.shape[0]):
        out_ref[i] = value


def log_sum(parts):
    top = jnp.max(parts, axis=0)
    return top + jnp.log2(jnp.sum(jnp.exp2(parts - top[None]), axis=0))


def row_sums(hot, values):
    total = None
    for _ in range(3):
        part = values.astype(BF16)
        values = values - part.astype(F32)
        product = jnp.dot(hot, part, preferred_element_type=F32)
        total = product if total is None else total + product
    return total


def by_half(parts_ref, half, slots):
    values = parts_ref[:, half * slots:(half + 1) * slots]
    return values.reshape(values.shape[0] * slots, LANES)


def first_samples(rows_hbm, cols_hbm, betas_hbm, energies_hbm, free_hbm, temps_hbm, counts_hbm,
                  out_ref, beta_ref, count_ref,
                  rows_ref, cols_ref, betas_ref, energies_ref, free_ref, temps_ref, counts_ref,
                  beta_cols, bias_cols, slot, total, sems):
    slots = energies_ref.shape[0]
    cut = energies_ref.shape[2] // LANES
    small = [
        pltpu.make_async_copy(source, target, sems.at[i])
        for i, (source, target) in enumerate([
            (temps_hbm, temps_ref), (counts_hbm, counts_ref), (free_hbm, free_ref),
            (betas_hbm, betas_ref), (cols_hbm, cols_ref), (rows_hbm, rows_ref),
        ])
    ]
    large = [
        pltpu.make_async_copy(
            energies_hbm.at[pl.ds(g * UNROLL, UNROLL)], energies_ref.at[pl.ds(g * UNROLL, UNROLL)],
            sems.at[len(small) + g],
        )
        for g in range(slots // UNROLL)
    ]
    for copy in small + large:
        copy.start()
    for copy in small:
        copy.wait()
    temps = temps_ref[...]
    beta = jnp.zeros(temps.shape, F32)
    for i in range(betas_ref.shape[0]):
        beta = jnp.where(temps == i, betas_ref[i], beta)
    count_ref[...] = LOG2E * jnp.log(counts_ref[...].astype(F32))
    beta_ref[...] = LOG2E * beta
    expand(beta_ref[...], beta_cols, 0.0)
    expand(count_ref[...] + LOG2E * free_ref[...], bias_cols, NEG)
    lane = lax.broadcasted_iota(jnp.int32, (1, LANES), 1)
    places = jnp.zeros((1, LANES), F32)
    for t in range(slots):
        places = jnp.where(lane == t, rows_ref[t].astype(F32), places)
    for g in range(slots // UNROLL):
        large[g].wait()
        for t in range(g * UNROLL, (g + 1) * UNROLL):
            beta, bias = beta_cols[cols_ref[t]], bias_cols[cols_ref[t]]
            for h, energy in enumerate(halves(energies_ref, t)):
                score = bias - beta * energy
                peak = jnp.max(score, axis=0, keepdims=True)
                slot[h * slots + t:h * slots + t + 1] = peak
                total[h * slots + t:h * slots + t + 1] = jnp.sum(jnp.exp2(score - peak), axis=0, keepdims=True)
    whole = slot[...] + jnp.log2(jnp.maximum(total[...], 1.0))
    for i in range(out_ref.shape[0]):
        out_ref[i, :cut * slots] = whole
        out_ref[i, cut * slots:] = jnp.broadcast_to(places, (8, LANES))


def first_states(rows_hbm, cols_hbm, beta_hbm, energies_ref, parts_ref, out_ref, drop_ref, hot_ref, beta_cols,
                 rows_ref, cols_ref, sems, beta_ref, top, total):
    index = [
        pltpu.make_async_copy(rows_hbm, rows_ref, sems.at[0]), pltpu.make_async_copy(cols_hbm, cols_ref, sems.at[1]),
        pltpu.make_async_copy(beta_hbm, beta_ref, sems.at[2]),
    ]
    for copy in index:
        copy.start()
    blocks = beta_cols.shape[0] - 1
    slots = energies_ref.shape[0]
    cut = energies_ref.shape[2] // LANES
    blocks_samp = drop_ref.shape[0] // cut
    wide = []
    for j in range(parts_ref.shape[0] * slots // LANES):
        places = jnp.zeros((1, LANES), F32)
        for i in range(LANES // slots):
            place = parts_ref[j * (LANES // slots) + i, cut * slots:cut * slots + 1]
            place = jnp.where(lax.broadcasted_iota(jnp.int32, place.shape, 1) < slots, place, 0.0)
            places = places + (pltpu.roll(place, i * slots, 1) if i else place)
        wide.append(places)
    wide = jnp.concatenate(wide, axis=1)
    row = lax.broadcasted_iota(jnp.int32, (blocks_samp, wide.shape[1]), 0).astype(F32)
    hot = jnp.where(row == wide, 1.0, 0.0).astype(BF16)
    hot_ref[...] = hot
    parts = jnp.concatenate([by_half(parts_ref, h, slots) for h in range(cut)], axis=1)
    step = jnp.clip(jnp.floor((parts - BASE) * (1.0 / STEP)), 0.0, LAST)
    power = jnp.exp2(BITS * step).astype(BF16)
    found = jnp.maximum(jnp.dot(hot, power, preferred_element_type=F32), 1.0)
    step = jnp.floor(jnp.log2(found) * (1.0 / BITS) + 0.03)
    back = lax.dot_general(hot, step.astype(BF16), (((0,), (0,)), ((), ())), preferred_element_type=F32)
    whole = row_sums(hot, jnp.exp2(parts - (BASE + STEP * back)))
    whole = BASE + STEP * step + jnp.log2(jnp.maximum(whole, 0.5))
    for h in range(cut):
        drop_ref[h * blocks_samp:(h + 1) * blocks_samp] = whole[:, h * LANES:(h + 1) * LANES]
    top[...] = jnp.full(top.shape, NEG, F32)
    total[...] = jnp.zeros(total.shape, F32)
    for copy in index:
        copy.wait()
    expand(beta_ref[...], beta_cols, 0.0)

    def drop_of(h, t):
        return drop_ref[pl.ds(h * blocks_samp + rows_ref[t], 1)]

    for t in range(slots):
        col = cols_ref[t]
        beta = beta_cols[col]
        most = top[col]
        for h, energy in enumerate(halves(energies_ref, t)):
            most = jnp.maximum(most, -(beta * energy) - drop_of(h, t))
        top[col] = most
    for c in range(blocks):
        top[c] = jnp.broadcast_to(jnp.max(top[c], axis=1, keepdims=True), top.shape[1:])
    for t in range(slots):
        col = cols_ref[t]
        beta, most = beta_cols[col], top[col]
        part = total[col]
        for h, energy in enumerate(halves(energies_ref, t)):
            part = part + jnp.exp2(-(beta * energy) - drop_of(h, t) - most)
        total[col] = part
    each = LANES // top.shape[1]
    lane = lax.broadcasted_iota(jnp.int32, (LANES, LANES), 1)
    tops = jnp.zeros((LANES, LANES), F32)
    sums = jnp.ones((LANES, LANES), F32)
    for j in range(blocks // each):
        column = range(each * j, each * j + each)
        tops = jnp.where(lane == j, jnp.concatenate([top[c] for c in column], axis=0), tops)
        sums = jnp.where(
            lane == j,
            jnp.concatenate([jnp.sum(total[c], axis=1, keepdims=True) for c in column], axis=0),
            sums,
        )
    rows = blocks // each
    out_ref[...] = tops.T[:rows] + jnp.log2(jnp.maximum(sums.T[:rows], 1.0))


def both_cores(parts_ref, out_ref):
    copies(out_ref, log_sum(parts_ref[...]))


def second_samples(rows_hbm, cols_hbm, energies_ref, beta_cols, count_ref, drop_ref, parts_ref,
                   out_ref, bias_cols, rows_ref, cols_ref, sems, slot):
    index = [
        pltpu.make_async_copy(rows_hbm, rows_ref, sems.at[0]), pltpu.make_async_copy(cols_hbm, cols_ref, sems.at[1])
    ]
    for copy in index:
        copy.start()
    slots = energies_ref.shape[0]
    cut = energies_ref.shape[2] // LANES
    blocks_samp = drop_ref.shape[0] // cut
    expand(count_ref[...] - log_sum(parts_ref[...]), bias_cols, NEG)
    for copy in index:
        copy.wait()
    for t in range(slots):
        beta, bias = beta_cols[cols_ref[t]], bias_cols[cols_ref[t]]
        for h, energy in enumerate(halves(energies_ref, t)):
            part = jnp.exp2(bias - beta * energy - drop_ref[pl.ds(h * blocks_samp + rows_ref[t], 1)])
            slot[h * slots + t:h * slots + t + 1] = jnp.maximum(
                jnp.sum(part, axis=0, keepdims=True), jnp.max(part, axis=0, keepdims=True)
            )
    copies(out_ref, slot[...])


def second_states(rows_hbm, cols_hbm, energies_ref, beta_cols, bias_cols, drop_ref, hot_ref, parts_ref, basis_ref,
                  out_ref, rows_ref, cols_ref, sems, drop, values):
    index = [
        pltpu.make_async_copy(rows_hbm, rows_ref, sems.at[0]), pltpu.make_async_copy(cols_hbm, cols_ref, sems.at[1])
    ]
    for copy in index:
        copy.start()
    blocks = beta_cols.shape[0] - 1
    slots = energies_ref.shape[0]
    count = basis_ref.shape[0]
    width = energies_ref.shape[2]
    cut = width // LANES
    blocks_samp = drop_ref.shape[0] // cut
    parts = jnp.concatenate([by_half(parts_ref, h, slots) for h in range(cut)], axis=1)
    whole = jnp.log2(jnp.maximum(row_sums(hot_ref[...], parts), TINY))
    for h in range(cut):
        here = slice(h * blocks_samp, (h + 1) * blocks_samp)
        drop[here] = drop_ref[here] + whole[:, h * LANES:(h + 1) * LANES]
    values[...] = jnp.zeros(values.shape, F32)
    ones = jnp.ones((values.shape[1] - count, width), BF16)
    for copy in index:
        copy.wait()
    for t in range(slots):
        row, col = rows_ref[t], cols_ref[t]
        beta, bias = beta_cols[col], bias_cols[col]
        weight = jnp.concatenate(
            [
                jnp.exp2(bias - beta * energy - drop[pl.ds(h * blocks_samp + row, 1)])
                for h, energy in enumerate(halves(energies_ref, t))
            ],
            axis=1,
        )
        high = weight.astype(BF16)
        low = (weight - high.astype(F32)).astype(BF16)
        factor = jnp.concatenate([basis_ref[:, pl.ds(pl.multiple_of(row * width, width), width)], ones], axis=0)
        dims = (((1,), (1,)), ((), ()))
        values[col] += lax.dot_general(factor, high, dims, preferred_element_type=F32) + lax.dot_general(
            factor, low, dims, preferred_element_type=F32
        )
    each = LANES // values.shape[2]
    across = blocks // each
    half = out_ref.shape[1] // 9
    for j in range(across):
        wide = jnp.concatenate([values[c] for c in range(each * j, each * j + each)], axis=1)
        for g in range(count // 8):
            owner = g * across + j
            start = owner % half * 9
            out_ref[owner // half, start:start + 8] = wide[8 * g:8 * g + 8]
            out_ref[owner // half, start + 8:start + 9] = wide[count:count + 1]


def core_sums(parts_ref, out_ref):
    mine = my_core()
    value = parts_ref[0, mine] + parts_ref[1, mine]
    for i in range(out_ref.shape[0]):
        for r in range(9):
            out_ref[i, r] = value[9 * i + r:9 * i + r + 1]


def finish(parts_ref, out_ref):
    both = jnp.sum(parts_ref[...], axis=0)
    value = jnp.concatenate([both[r] for r in range(8)], axis=0)
    copies(out_ref, value / both[8])


def spread(parts, axis):
    return lax.all_to_all(parts, axis, 0, 0)


def pair(parts):
    return lax.all_gather(parts, "core")


def my_core():
    return lax.axis_index("core")


def call(kernel, out_shape, in_specs, scratch_shapes=(), limit=40 * MIB):
    single = not isinstance(out_shape, tuple)
    return pl.pallas_call(
        kernel,
        out_shape=out_shape,
        in_specs=in_specs,
        out_specs=vmem(1)[0] if single else tuple(vmem(len(out_shape))),
        scratch_shapes=list(scratch_shapes),
        compiler_params=pltpu.CompilerParams(vmem_limit_bytes=limit),
    )


def on_device(n_core, n_z, n_state, energies, tile_rows, tile_cols, start_free, temps, betas, counts, basis):
    slots, state_block, sample_block = energies.shape
    state_dev = start_free.shape[0]
    blocks = state_dev // state_block
    blocks_samp = basis.shape[1] // sample_block
    cut = sample_block // LANES
    rows = state_dev // LANES
    count = basis.shape[0]
    shape = lambda *dims: jax.ShapeDtypeStruct(dims, F32)
    by_state = (blocks + 1, state_block, LANES)
    place = [
        pltpu.SMEM(tile_rows.shape, jnp.int32), pltpu.SMEM(tile_cols.shape, jnp.int32), pltpu.SemaphoreType.DMA((3,))
    ]
    flat = pltpu.VMEM((rows, LANES), F32)
    whole = pltpu.VMEM((rows, LANES), jnp.int32)
    by_slot = pltpu.VMEM((cut * slots, LANES), F32)

    parts, beta, log_count = call(
        first_samples,
        (shape(n_state, cut * slots + 8, LANES), shape(rows, LANES), shape(rows, LANES)),
        hbm(7),
        place[:2] + [
            pltpu.SMEM(betas.shape, F32),
            pltpu.VMEM(energies.shape, F32),
            flat, whole, whole, pltpu.VMEM(by_state, F32), pltpu.VMEM(by_state, F32), by_slot, by_slot,
            pltpu.SemaphoreType.DMA((6 + slots // UNROLL,)),
        ],
        FIRST_VMEM,
    )(
        tile_rows, tile_cols, betas, energies,
        start_free.reshape(rows, LANES), temps.reshape(rows, LANES), counts.reshape(rows, LANES),
    )
    parts = spread(parts, "state")
    parts, drop, hot, beta_cols = call(
        first_states,
        (
            shape(rows, LANES), shape(cut * blocks_samp, LANES),
            jax.ShapeDtypeStruct((blocks_samp, n_state * slots), BF16), shape(*by_state),
        ),
        anywhere(3) + vmem(2),
        place + [flat, pltpu.VMEM(by_state, F32), pltpu.VMEM(by_state, F32)],
    )(tile_rows, tile_cols, beta, energies, parts)
    parts = pair(parts)
    parts = call(both_cores, shape(n_z, rows, LANES), vmem(1))(parts)
    parts = spread(parts, "z")
    parts, bias = call(
        second_samples,
        (shape(n_state, cut * slots, LANES), shape(*by_state)),
        anywhere(2) + vmem(5),
        place + [by_slot],
    )(tile_rows, tile_cols, energies, beta_cols, log_count, drop, parts)
    parts = spread(parts, "state")
    parts = call(
        second_states,
        shape(n_core, n_z * 9, LANES),
        anywhere(2) + vmem(7),
        place + [
            pltpu.VMEM((cut * blocks_samp, LANES), F32), pltpu.VMEM((blocks + 1, count + 16, state_block), F32)
        ],
    )(tile_rows, tile_cols, energies, beta_cols, bias, drop, hot, parts, basis)
    parts = pair(parts)
    parts = call(core_sums, shape(n_z, 9, 1, LANES), vmem(1))(parts)
    parts = spread(parts, "z")
    parts = call(finish, shape(n_z, 8, LANES), vmem(1))(parts)
    parts = spread(parts, "z")
    parts = pair(parts)
    return parts.reshape(count // 8, rows, 8, LANES).transpose(0, 2, 1, 3).reshape(count, state_dev)


def solution(mesh):
    n_samp, n_state = mesh.shape["samp"], mesh.shape["state"]
    n_core = 2
    n_z = n_samp // n_core
    cut = Mesh(mesh.devices.reshape(n_z, n_core, n_state), ("z", "core", "state"))
    samp = ("z", "core")

    def run(*args):
        return on_device(n_core, n_z, n_state, *args)

    return jax.shard_map(
        run,
        mesh=cut,
        in_specs=(
            P(("z", "core", "state"), None, None),
            P(("z", "core", "state")),
            P(("z", "core", "state")),
            P("state"),
            P("state"),
            P(),
            P("state"),
            P(None, samp),
        ),
        out_specs=P(None, "state"),
        check_vma=False,
    )
```

time: 116 us -> 111 us (0.957)
  local copies, waits for them, and re-layouts: 6.6 us -> 1.36 us
    unnamed x23 -> x13, local copies, waits for them, and re-layouts: 6.29 us -> 1.36 us
    all_to_all x5, blocking collectives: 88.7 us -> 86.3 us  [spread(): return lax.all_to_all(parts, axis, 0, 0)]
    all_gather x3, blocking collectives: 11.9 us -> 14.3 us  [pair(): return lax.all_gather(parts, 'core')]
    pallas_call x1, Pallas kernels: 1.62 us -> 3.03 us  [on_device(): call(first_samples, (shape(n_state, cut * slots + 8, LANES), shape(rows,...]
where the time goes in v3:
time: 111 us
  blocking collectives  101 us (91%)
  Pallas kernels  8.47 us (8%)
  local copies, waits for them, and re-layouts  1.36 us (1%)
    all_to_all x5, blocking collectives, spread(): return lax.all_to_all(parts, axis, 0, 0)  86.3 us
    all_gather x3, blocking collectives, pair(): return lax.all_gather(parts, 'core')  14.3 us
    pallas_call x1, Pallas kernels, on_device(): call(first_samples, (shape(n_state, cut * slots + 8, LANES), shape(rows,...  3.03 us
    pallas_call x1, Pallas kernels, on_device(): call(first_states, (shape(rows, LANES), shape(cut * blocks_samp, LANES),...  2.59 us

profile of v3, /device:TPU:1, one launch (start us, length us, event | category | flops | bytes accessed | tf_op | source)
XLA Modules:
  0.0 110.6 jit_solution(14627296256003793593)
XLA Ops:
  0.0 0.0 copy-start.3
  0.0 0.0 copy-start.2
  0.0 0.0 copy-start
  0.0 3.0 %shard_map.82 = (f32[16,72,128]{2,1,0:T(8,128)}, f32[8,128]{1,0:T(8,128)}, f32[8,128]{1,0:T(8,128)}) custom-call(s32[32]{0:T(128)} %rows_hbm.7, s32[32]{0:T(128)} %cols_hbm.7, f32[16]{0:T(128)} %betas_hbm.1, f32[32,64,256]{2,1,0:T(8,128)} %energies_ref.5, f32[8,128]{1,0:T(8,128)} %bitcast.13, s32[8,128]{1,0:T(8,128)} %bitcast.14, s32[8,128]{1,0:T(8,128)} %bitcast.15), custom_call_target="tpu_custom_call" | custom-call | tf_op jit(solution)/shard_map/pallas_call | solution.py:339
  3.0 0.0 copy-start.4
  3.1 17.0 %all_to_all.25.parts_ref = f32[16,72,128]{2,1,0:T(8,128)S(1)} all-to-all(f32[16,72,128]{2,1,0:T(8,128)} %get-tuple-element.15), channel_id=1, replica_groups=mesh['z'=16,'core'=2,'state'=16] {'state'}, dimensions={0} | all-to-all | bytes 1179648 | tf_op jit(solution)/shard_map/all_to_all | solution.py:299
  20.1 0.0 copy-done.3
  20.1 0.0 copy-done.2
  20.1 0.0 copy-done
  20.1 0.0 copy-start.5
  20.1 0.7 copy-done.5
  20.8 2.6 %shard_map.83 = (f32[8,128]{1,0:T(8,128)S(1)}, f32[128,128]{1,0:T(8,128)S(1)}, bf16[64,512]{1,0:T(8,128)(2,1)S(1)}, f32[17,64,128]{2,1,0:T(8,128)S(1)}) custom-call(s32[32]{0:T(128)S(1)} %copy-done.2, s32[32]{0:T(128)S(1)} %copy-done.3, f32[8,128]{1,0:T(8,128)S(1)} %copy-done.5, f32[32,64,256]{2,1,0:T(8,128)S(1)} %copy-done, ...), custom_call_target="tpu_custom_call" | custom-call | tf_op jit(solution)/shard_map/pallas_call | solution.py:355
  23.4 0.0 copy-start.1
  23.4 5.4 %all-gather = f32[16,128]{1,0:T(8,128)S(1)} all-gather(f32[8,128]{1,0:T(8,128)S(1)} %get-tuple-element.19), channel_id=2, replica_groups=mesh['z'=16,'core'=2,'state'=16] {'core'}, dimensions={0}, use_global_device_ids=true | all-gather | bytes 12288 | tf_op jit(solution)/shard_map/all_gather | solution.py:303
  28.9 26.3 %all_to_all.26.parts_ref = f32[16,8,128]{2,1,0:T(8,128)S(1)} all-to-all(f32[16,8,128]{2,1,0:T(8,128)S(1)} %shard_map.84), channel_id=1, replica_groups=mesh['z'=16,'core'=2,'state'=16] {'z'}, dimensions={0} | all-to-all | bytes 131072 | tf_op jit(solution)/shard_map/all_to_all | solution.py:299
  55.1 0.0 copy-done.4
  55.1 1.2 %shard_map.85 = (f32[16,64,128]{2,1,0:T(8,128)S(1)}, f32[17,64,128]{2,1,0:T(8,128)S(1)}) custom-call(s32[32]{0:T(128)S(1)} %copy-done.2, s32[32]{0:T(128)S(1)} %copy-done.3, f32[32,64,256]{2,1,0:T(8,128)S(1)} %copy-done, f32[17,64,128]{2,1,0:T(8,128)S(1)} %get-tuple-element.16.beta_cols, f32[8,128]{1,0:T(8,128)S(1)} %copy-done.4, ...), custom_call_target="tpu_custom_call" | custom-call | tf_op jit(solution)/shard_map/pallas_call | solution.py:367
  56.3 12.2 %all_to_all.27.parts_ref = f32[16,64,128]{2,1,0:T(8,128)S(1)} all-to-all(f32[16,64,128]{2,1,0:T(8,128)S(1)} %get-tuple-element.22), channel_id=1, replica_groups=mesh['z'=16,'core'=2,'state'=16] {'state'}, dimensions={0} | all-to-all | bytes 1048576 | tf_op jit(solution)/shard_map/all_to_all | solution.py:299
  68.5 0.0 copy-done.1
  68.5 1.6 %shard_map.86 = f32[2,144,128]{2,1,0:T(8,128)S(1)} custom-call(s32[32]{0:T(128)S(1)} %copy-done.2, s32[32]{0:T(128)S(1)} %copy-done.3, f32[32,64,256]{2,1,0:T(8,128)S(1)} %copy-done, f32[17,64,128]{2,1,0:T(8,128)S(1)} %get-tuple-element.16.beta_cols, f32[17,64,128]{2,1,0:T(8,128)S(1)} %get-tuple-element.20.bias_cols, ...), custom_call_target="tpu_custom_call" | custom-call | tf_op jit(solution)/shard_map/pallas_call | solution.py:374
  70.1 4.9 %all-gather.1 = f32[4,144,128]{2,1,0:T(8,128)S(1)} all-gather(f32[2,144,128]{2,1,0:T(8,128)S(1)} %shard_map.86), channel_id=3, replica_groups=mesh['z'=16,'core'=2,'state'=16] {'core'}, dimensions={0}, use_global_device_ids=true | all-gather | bytes 442368 | tf_op jit(solution)/shard_map/all_gather | solution.py:303
  75.0 15.4 %all_to_all.28.parts_ref = f32[16,9,1,128]{3,2,1,0:T(1,128)S(1)} all-to-all(f32[16,9,1,128]{3,2,1,0:T(1,128)S(1)} %shard_map.87), channel_id=1, replica_groups=mesh['z'=16,'core'=2,'state'=16] {'z'}, dimensions={0} | all-to-all | bytes 147456 | tf_op jit(solution)/shard_map/all_to_all | solution.py:299
  90.5 0.1 shard_map.88
  90.5 15.4 %all_to_all.29 = f32[16,8,128]{2,1,0:T(8,128)S(1)} all-to-all(f32[16,8,128]{2,1,0:T(8,128)S(1)} %shard_map.88), channel_id=1, replica_groups=mesh['z'=16,'core'=2,'state'=16] {'z'}, dimensions={0} | all-to-all | bytes 131072 | tf_op jit(solution)/shard_map/all_to_all | solution.py:299
  105.9 4.0 %all-gather.2 = f32[32,8,128]{2,1,0:T(8,128)S(1)} all-gather(f32[16,8,128]{2,1,0:T(8,128)S(1)} %all_to_all.29), channel_id=4, replica_groups=mesh['z'=16,'core'=2,'state'=16] {'core'}, dimensions={0}, use_global_device_ids=true | all-gather | bytes 196608 | tf_op jit(solution)/shard_map/all_gather | solution.py:303
  109.9 0.7 copy.10
  (2 shorter events, 0.0 us)
Async XLA Ops:
  0.0 20.1 %copy-start.3 = (s32[32]{0:T(128)S(1)}, s32[32]{0:T(128)}, u32[]{:S(2)}) copy-start(s32[32]{0:T(128)} %cols_hbm.7) | copy-start | bytes 388
  0.0 20.1 %copy-start.2 = (s32[32]{0:T(128)S(1)}, s32[32]{0:T(128)}, u32[]{:S(2)}) copy-start(s32[32]{0:T(128)} %rows_hbm.7) | copy-start | bytes 388
  0.0 20.1 %copy-start = (f32[32,64,256]{2,1,0:T(8,128)S(1)}, f32[32,64,256]{2,1,0:T(8,128)}, u32[]{:S(2)}) copy-start(f32[32,64,256]{2,1,0:T(8,128)} %energies_ref.5) | copy-start | bytes 6291460
  3.0 52.1 %copy-start.4 = (f32[8,128]{1,0:T(8,128)S(1)}, f32[8,128]{1,0:T(8,128)}, u32[]{:S(2)}) copy-start(f32[8,128]{1,0:T(8,128)} %get-tuple-element.17.count_ref) | copy-start | bytes 12292
  20.1 0.7 copy-start.5
  23.4 45.1 %copy-start.1 = (bf16[32,16384]{1,0:T(8,128)(2,1)S(1)}, bf16[32,16384]{1,0:T(8,128)(2,1)}, u32[]{:S(2)}) copy-start(bf16[32,16384]{1,0:T(8,128)(2,1)} %basis_ref.1) | copy-start | bytes 3145732

commit v4 on v3

--- a/solution.py
+++ b/solution.py
@@ -36,6 +36,17 @@
     return [pl.BlockSpec(memory_space=pl.ANY)] * count
 
 
+def state_beta(temps, betas_ref):
+    beta = jnp.zeros(temps.shape, F32)
+    for i in range(betas_ref.shape[0]):
+        beta = jnp.where(temps == i, betas_ref[i], beta)
+    return -LOG2E * beta
+
+
+def log_count(counts_ref):
+    return LOG2E * jnp.log(counts_ref[...].astype(F32))
+
+
 def expand(rows, cols_ref, spare):
     turned = rows.T
     size = cols_ref.shape[1]
@@ -78,7 +89,7 @@
 
 
 def first_samples(rows_hbm, cols_hbm, betas_hbm, energies_hbm, free_hbm, temps_hbm, counts_hbm,
-                  out_ref, beta_ref, count_ref,
+                  out_ref,
                   rows_ref, cols_ref, betas_ref, energies_ref, free_ref, temps_ref, counts_ref,
                   beta_cols, bias_cols, slot, total, sems):
     slots = energies_ref.shape[0]
@@ -101,14 +112,8 @@
         copy.start()
     for copy in small:
         copy.wait()
-    temps = temps_ref[...]
-    beta = jnp.zeros(temps.shape, F32)
-    for i in range(betas_ref.shape[0]):
-        beta = jnp.where(temps == i, betas_ref[i], beta)
-    count_ref[...] = LOG2E * jnp.log(counts_ref[...].astype(F32))
-    beta_ref[...] = LOG2E * beta
-    expand(beta_ref[...], beta_cols, 0.0)
-    expand(count_ref[...] + LOG2E * free_ref[...], bias_cols, NEG)
+    expand(state_beta(temps_ref[...], betas_ref), beta_cols, 0.0)
+    expand(log_count(counts_ref) + LOG2E * free_ref[...], bias_cols, NEG)
     lane = lax.broadcasted_iota(jnp.int32, (1, LANES), 1)
     places = jnp.zeros((1, LANES), F32)
     for t in range(slots):
@@ -118,7 +123,7 @@
         for t in range(g * UNROLL, (g + 1) * UNROLL):
             beta, bias = beta_cols[cols_ref[t]], bias_cols[cols_ref[t]]
             for h, energy in enumerate(halves(energies_ref, t)):
-                score = bias - beta * energy
+                score = bias + beta * energy
                 peak = jnp.max(score, axis=0, keepdims=True)
                 slot[h * slots + t:h * slots + t + 1] = peak
                 total[h * slots + t:h * slots + t + 1] = jnp.sum(jnp.exp2(score - peak), axis=0, keepdims=True)
@@ -128,18 +133,18 @@
         out_ref[i, cut * slots:] = jnp.broadcast_to(places, (8, LANES))
 
 
-def first_states(rows_hbm, cols_hbm, beta_hbm, energies_ref, parts_ref, out_ref, drop_ref, hot_ref, beta_cols,
-                 rows_ref, cols_ref, sems, beta_ref, top, total):
+def first_states(rows_hbm, cols_hbm, betas_hbm, temps_ref, energies_ref, parts_ref, out_ref, values_ref, hot_ref,
+                 rows_ref, cols_ref, sems, betas_ref, beta_cols, drop, top, total):
     index = [
         pltpu.make_async_copy(rows_hbm, rows_ref, sems.at[0]), pltpu.make_async_copy(cols_hbm, cols_ref, sems.at[1]),
-        pltpu.make_async_copy(beta_hbm, beta_ref, sems.at[2]),
+        pltpu.make_async_copy(betas_hbm, betas_ref, sems.at[2]),
     ]
     for copy in index:
         copy.start()
     blocks = beta_cols.shape[0] - 1
     slots = energies_ref.shape[0]
     cut = energies_ref.shape[2] // LANES
-    blocks_samp = drop_ref.shape[0] // cut
+    blocks_samp = drop.shape[0] // cut
     wide = []
     for j in range(parts_ref.shape[0] * slots // LANES):
         places = jnp.zeros((1, LANES), F32)
@@ -161,31 +166,30 @@
     whole = row_sums(hot, jnp.exp2(parts - (BASE + STEP * back)))
     whole = BASE + STEP * step + jnp.log2(jnp.maximum(whole, 0.5))
     for h in range(cut):
-        drop_ref[h * blocks_samp:(h + 1) * blocks_samp] = whole[:, h * LANES:(h + 1) * LANES]
+        drop[h * blocks_samp:(h + 1) * blocks_samp] = whole[:, h * LANES:(h + 1) * LANES]
     top[...] = jnp.full(top.shape, NEG, F32)
     total[...] = jnp.zeros(total.shape, F32)
     for copy in index:
         copy.wait()
-    expand(beta_ref[...], beta_cols, 0.0)
-
-    def drop_of(h, t):
-        return drop_ref[pl.ds(h * blocks_samp + rows_ref[t], 1)]
+    expand(state_beta(temps_ref[...], betas_ref), beta_cols, 0.0)
 
     for t in range(slots):
-        col = cols_ref[t]
+        row, col = rows_ref[t], cols_ref[t]
         beta = beta_cols[col]
         most = top[col]
         for h, energy in enumerate(halves(energies_ref, t)):
-            most = jnp.maximum(most, -(beta * energy) - drop_of(h, t))
+            value = beta * energy - drop[pl.ds(h * blocks_samp + row, 1)]
+            values_ref[t, :, h * LANES:(h + 1) * LANES] = value
+            most = jnp.maximum(most, value)
         top[col] = most
     for c in range(blocks):
         top[c] = jnp.broadcast_to(jnp.max(top[c], axis=1, keepdims=True), top.shape[1:])
     for t in range(slots):
         col = cols_ref[t]
-        beta, most = beta_cols[col], top[col]
+        most = top[col]
         part = total[col]
-        for h, energy in enumerate(halves(energies_ref, t)):
-            part = part + jnp.exp2(-(beta * energy) - drop_of(h, t) - most)
+        for value in halves(values_ref, t):
+            part = part + jnp.exp2(value - most)
         total[col] = part
     each = LANES // top.shape[1]
     lane = lax.broadcasted_iota(jnp.int32, (LANES, LANES), 1)
@@ -207,73 +211,62 @@
     copies(out_ref, log_sum(parts_ref[...]))
 
 
-def second_samples(rows_hbm, cols_hbm, energies_ref, beta_cols, count_ref, drop_ref, parts_ref,
-                   out_ref, bias_cols, rows_ref, cols_ref, sems, slot):
+def second_samples(cols_hbm, values_ref, counts_ref, parts_ref, out_ref, weights_ref,
+                   cols_ref, sem, bias_cols, slot):
+    copy = pltpu.make_async_copy(cols_hbm, cols_ref, sem)
+    copy.start()
+    slots = values_ref.shape[0]
+    expand(log_count(counts_ref) - log_sum(parts_ref[...]), bias_cols, NEG)
+    copy.wait()
+    for t in range(slots):
+        bias = bias_cols[cols_ref[t]]
+        for h, value in enumerate(halves(values_ref, t)):
+            part = jnp.exp2(bias + value)
+            weights_ref[t, :, h * LANES:(h + 1) * LANES] = part
+            slot[h * slots + t:h * slots + t + 1] = jnp.maximum(
+                jnp.sum(part, axis=0, keepdims=True), jnp.max(part, axis=0, keepdims=True)
+            )
+    copies(out_ref, slot[...])
+
+
+def second_states(rows_hbm, cols_hbm, weights_ref, hot_ref, parts_ref, basis_ref, out_ref,
+                  rows_ref, cols_ref, sems, scale, sums):
     index = [
         pltpu.make_async_copy(rows_hbm, rows_ref, sems.at[0]), pltpu.make_async_copy(cols_hbm, cols_ref, sems.at[1])
     ]
     for copy in index:
         copy.start()
-    slots = energies_ref.shape[0]
-    cut = energies_ref.shape[2] // LANES
-    blocks_samp = drop_ref.shape[0] // cut
-    expand(count_ref[...] - log_sum(parts_ref[...]), bias_cols, NEG)
-    for copy in index:
-        copy.wait()
-    for t in range(slots):
-        beta, bias = beta_cols[cols_ref[t]], bias_cols[cols_ref[t]]
-        for h, energy in enumerate(halves(energies_ref, t)):
-            part = jnp.exp2(bias - beta * energy - drop_ref[pl.ds(h * blocks_samp + rows_ref[t], 1)])
-            slot[h * slots + t:h * slots + t + 1] = jnp.maximum(
-                jnp.sum(part, axis=0, keepdims=True), jnp.max(part, axis=0, keepdims=True)
-            )
-    copies(out_ref, slot[...])
-
-
-def second_states(rows_hbm, cols_hbm, energies_ref, beta_cols, bias_cols, drop_ref, hot_ref, parts_ref, basis_ref,
-                  out_ref, rows_ref, cols_ref, sems, drop, values):
-    index = [
-        pltpu.make_async_copy(rows_hbm, rows_ref, sems.at[0]), pltpu.make_async_copy(cols_hbm, cols_ref, sems.at[1])
-    ]
-    for copy in index:
-        copy.start()
-    blocks = beta_cols.shape[0] - 1
-    slots = energies_ref.shape[0]
+    blocks = sums.shape[0] - 1
+    slots = weights_ref.shape[0]
     count = basis_ref.shape[0]
-    width = energies_ref.shape[2]
+    width = weights_ref.shape[2]
     cut = width // LANES
-    blocks_samp = drop_ref.shape[0] // cut
+    blocks_samp = scale.shape[0] // cut
     parts = jnp.concatenate([by_half(parts_ref, h, slots) for h in range(cut)], axis=1)
-    whole = jnp.log2(jnp.maximum(row_sums(hot_ref[...], parts), TINY))
+    whole = 1.0 / jnp.maximum(row_sums(hot_ref[...], parts), TINY)
     for h in range(cut):
-        here = slice(h * blocks_samp, (h + 1) * blocks_samp)
-        drop[here] = drop_ref[here] + whole[:, h * LANES:(h + 1) * LANES]
-    values[...] = jnp.zeros(values.shape, F32)
-    ones = jnp.ones((values.shape[1] - count, width), BF16)
+        scale[h * blocks_samp:(h + 1) * blocks_samp] = whole[:, h * LANES:(h + 1) * LANES]
+    sums[...] = jnp.zeros(sums.shape, F32)
+    ones = jnp.ones((sums.shape[1] - count, width), BF16)
     for copy in index:
         copy.wait()
     for t in range(slots):
         row, col = rows_ref[t], cols_ref[t]
-        beta, bias = beta_cols[col], bias_cols[col]
         weight = jnp.concatenate(
-            [
-                jnp.exp2(bias - beta * energy - drop[pl.ds(h * blocks_samp + row, 1)])
-                for h, energy in enumerate(halves(energies_ref, t))
-            ],
-            axis=1,
+            [part * scale[pl.ds(h * blocks_samp + row, 1)] for h, part in enumerate(halves(weights_ref, t))], axis=1
         )
         high = weight.astype(BF16)
         low = (weight - high.astype(F32)).astype(BF16)
         factor = jnp.concatenate([basis_ref[:, pl.ds(pl.multiple_of(row * width, width), width)], ones], axis=0)
         dims = (((1,), (1,)), ((), ()))
-        values[col] += lax.dot_general(factor, high, dims, preferred_element_type=F32) + lax.dot_general(
+        sums[col] += lax.dot_general(factor, high, dims, preferred_element_type=F32) + lax.dot_general(
             factor, low, dims, preferred_element_type=F32
         )
-    each = LANES // values.shape[2]
+    each = LANES // sums.shape[2]
     across = blocks // each
     half = out_ref.shape[1] // 9
     for j in range(across):
-        wide = jnp.concatenate([values[c] for c in range(each * j, each * j + each)], axis=1)
+        wide = jnp.concatenate([sums[c] for c in range(each * j, each * j + each)], axis=1)
         for g in range(count // 8):
             owner = g * across + j
             start = owner % half * 9
@@ -295,16 +288,16 @@
     copies(out_ref, value / both[8])
 
 
+def my_core():
+    return lax.axis_index("core")
+
+
 def spread(parts, axis):
     return lax.all_to_all(parts, axis, 0, 0)
 
 
 def pair(parts):
     return lax.all_gather(parts, "core")
-
-
-def my_core():
-    return lax.axis_index("core")
 
 
 def call(kernel, out_shape, in_specs, scratch_shapes=(), limit=40 * MIB):
@@ -336,9 +329,11 @@
     whole = pltpu.VMEM((rows, LANES), jnp.int32)
     by_slot = pltpu.VMEM((cut * slots, LANES), F32)
 
-    parts, beta, log_count = call(
+    free, temps, counts = (vector.reshape(rows, LANES) for vector in (start_free, temps, counts))
+
+    parts = call(
         first_samples,
-        (shape(n_state, cut * slots + 8, LANES), shape(rows, LANES), shape(rows, LANES)),
+        shape(n_state, cut * slots + 8, LANES),
         hbm(7),
         place[:2] + [
             pltpu.SMEM(betas.shape, F32),
@@ -347,38 +342,38 @@
             pltpu.SemaphoreType.DMA((6 + slots // UNROLL,)),
         ],
         FIRST_VMEM,
-    )(
-        tile_rows, tile_cols, betas, energies,
-        start_free.reshape(rows, LANES), temps.reshape(rows, LANES), counts.reshape(rows, LANES),
-    )
+    )(tile_rows, tile_cols, betas, energies, free, temps, counts)
     parts = spread(parts, "state")
-    parts, drop, hot, beta_cols = call(
+    parts, values, hot = call(
         first_states,
         (
-            shape(rows, LANES), shape(cut * blocks_samp, LANES),
-            jax.ShapeDtypeStruct((blocks_samp, n_state * slots), BF16), shape(*by_state),
+            shape(rows, LANES), shape(*energies.shape),
+            jax.ShapeDtypeStruct((blocks_samp, n_state * slots), BF16),
         ),
-        anywhere(3) + vmem(2),
-        place + [flat, pltpu.VMEM(by_state, F32), pltpu.VMEM(by_state, F32)],
-    )(tile_rows, tile_cols, beta, energies, parts)
+        anywhere(3) + vmem(3),
+        place + [
+            pltpu.SMEM(betas.shape, F32), pltpu.VMEM(by_state, F32), pltpu.VMEM((cut * blocks_samp, LANES), F32),
+            pltpu.VMEM(by_state, F32), pltpu.VMEM(by_state, F32),
+        ],
+    )(tile_rows, tile_cols, betas, temps, energies, parts)
     parts = pair(parts)
     parts = call(both_cores, shape(n_z, rows, LANES), vmem(1))(parts)
     parts = spread(parts, "z")
-    parts, bias = call(
+    parts, weights = call(
         second_samples,
-        (shape(n_state, cut * slots, LANES), shape(*by_state)),
-        anywhere(2) + vmem(5),
-        place + [by_slot],
-    )(tile_rows, tile_cols, energies, beta_cols, log_count, drop, parts)
+        (shape(n_state, cut * slots, LANES), shape(*energies.shape)),
+        anywhere(1) + vmem(3),
+        [place[1], pltpu.SemaphoreType.DMA, pltpu.VMEM(by_state, F32), by_slot],
+    )(tile_cols, values, counts, parts)
     parts = spread(parts, "state")
     parts = call(
         second_states,
         shape(n_core, n_z * 9, LANES),
-        anywhere(2) + vmem(7),
+        anywhere(2) + vmem(4),
         place + [
             pltpu.VMEM((cut * blocks_samp, LANES), F32), pltpu.VMEM((blocks + 1, count + 16, state_block), F32)
         ],
-    )(tile_rows, tile_cols, energies, beta_cols, bias, drop, hot, parts, basis)
+    )(tile_rows, tile_cols, weights, hot, parts, basis)
     parts = pair(parts)
     parts = call(core_sums, shape(n_z, 9, 1, LANES), vmem(1))(parts)
     parts = spread(parts, "z")

time: 111 us -> 110 us (level)
  no operation moved by 1% of the time
where the time goes in v4:
time: 110 us
  blocking collectives  101 us (92%)
  Pallas kernels  8.23 us (7%)
    all_to_all x5, blocking collectives, spread(): return lax.all_to_all(parts, axis, 0, 0)  86.3 us
    all_gather x3, blocking collectives, pair(): return lax.all_gather(parts, 'core')  14.3 us
    pallas_call x1, Pallas kernels, on_device(): call(first_samples, shape(n_state, cut * slots + 8, LANES), hbm(7), place...  3.02 us
    pallas_call x1, Pallas kernels, on_device(): call(first_states, (shape(rows, LANES), shape(*energies.shape), jax.Shape...  2.59 us

profile of v4, /device:TPU:1, one launch (start us, length us, event | category | flops | bytes accessed | tf_op | source)
XLA Modules:
  0.0 109.7 jit_solution(5954111008968670889)
XLA Ops:
  0.0 0.0 copy-start.4
  0.0 0.0 copy-start.5
  0.0 0.0 copy-start.6
  0.0 0.0 copy-start
  0.0 0.0 copy-start.2
  0.0 3.0 %shard_map.82 = f32[16,72,128]{2,1,0:T(8,128)} custom-call(s32[32]{0:T(128)} %rows_hbm.5, s32[32]{0:T(128)} %cols_hbm.7, f32[16]{0:T(128)} %betas_hbm.3, f32[32,64,256]{2,1,0:T(8,128)} %energies_ref.1, f32[8,128]{1,0:T(8,128)} %bitcast.17, s32[8,128]{1,0:T(8,128)} %bitcast.12, s32[8,128]{1,0:T(8,128)} %bitcast.14), custom_call_target="tpu_custom_call" | custom-call | tf_op jit(solution)/shard_map/pallas_call | solution.py:334
  3.1 0.0 copy-start.3
  3.1 17.0 %all_to_all.25.parts_ref = f32[16,72,128]{2,1,0:T(8,128)S(1)} all-to-all(f32[16,72,128]{2,1,0:T(8,128)} %shard_map.82), channel_id=1, replica_groups=mesh['z'=16,'core'=2,'state'=16] {'state'}, dimensions={0} | all-to-all | bytes 1179648 | tf_op jit(solution)/shard_map/all_to_all | solution.py:296
  20.1 0.0 copy-done.4
  20.1 0.0 copy-done.5
  20.1 0.0 copy-done.6
  20.1 0.0 copy-done
  20.1 0.0 copy-done.2
  20.1 2.6 %shard_map.83 = (f32[8,128]{1,0:T(8,128)S(1)}, f32[32,64,256]{2,1,0:T(8,128)S(1)}, bf16[64,512]{1,0:T(8,128)(2,1)S(1)}) custom-call(s32[32]{0:T(128)S(1)} %copy-done.5, s32[32]{0:T(128)S(1)} %copy-done.4, f32[16]{0:T(128)S(1)} %copy-done.6, s32[8,128]{1,0:T(8,128)S(1)} %bitcast.13, f32[32,64,256]{2,1,0:T(8,128)S(1)} %copy-done, ...), custom_call_target="tpu_custom_call" | custom-call | tf_op jit(solution)/shard_map/pallas_call | solution.py:347
  22.7 0.0 copy-start.1
  22.8 5.5 %all-gather = f32[16,128]{1,0:T(8,128)S(1)} all-gather(f32[8,128]{1,0:T(8,128)S(1)} %get-tuple-element.11), channel_id=2, replica_groups=mesh['z'=16,'core'=2,'state'=16] {'core'}, dimensions={0}, use_global_device_ids=true | all-gather | bytes 12288 | tf_op jit(solution)/shard_map/all_gather | solution.py:300
  28.2 26.3 %all_to_all.26.parts_ref = f32[16,8,128]{2,1,0:T(8,128)S(1)} all-to-all(f32[16,8,128]{2,1,0:T(8,128)S(1)} %shard_map.84), channel_id=1, replica_groups=mesh['z'=16,'core'=2,'state'=16] {'z'}, dimensions={0} | all-to-all | bytes 131072 | tf_op jit(solution)/shard_map/all_to_all | solution.py:296
  54.5 0.0 copy-done.3
  54.5 1.0 shard_map.85
  55.5 12.2 %all_to_all.27.parts_ref = f32[16,64,128]{2,1,0:T(8,128)S(1)} all-to-all(f32[16,64,128]{2,1,0:T(8,128)S(1)} %get-tuple-element.14), channel_id=1, replica_groups=mesh['z'=16,'core'=2,'state'=16] {'state'}, dimensions={0} | all-to-all | bytes 1048576 | tf_op jit(solution)/shard_map/all_to_all | solution.py:296
  67.7 0.0 copy-done.1
  67.7 1.6 %shard_map.86 = f32[2,144,128]{2,1,0:T(8,128)S(1)} custom-call(s32[32]{0:T(128)S(1)} %copy-done.5, s32[32]{0:T(128)S(1)} %copy-done.4, f32[32,64,256]{2,1,0:T(8,128)S(1)} %get-tuple-element.12.weights_ref, bf16[64,512]{1,0:T(8,128)(2,1)S(1)} %get-tuple-element.13.hot_ref, f32[16,64,128]{2,1,0:T(8,128)S(1)} %all_to_all.27.parts_ref, ...), custom_call_target="tpu_custom_call" | custom-call | tf_op jit(solution)/shard_map/pallas_call | solution.py:369
  69.2 4.9 %all-gather.1 = f32[4,144,128]{2,1,0:T(8,128)S(1)} all-gather(f32[2,144,128]{2,1,0:T(8,128)S(1)} %shard_map.86), channel_id=3, replica_groups=mesh['z'=16,'core'=2,'state'=16] {'core'}, dimensions={0}, use_global_device_ids=true | all-gather | bytes 442368 | tf_op jit(solution)/shard_map/all_gather | solution.py:300
  74.2 15.4 %all_to_all.28.parts_ref = f32[16,9,1,128]{3,2,1,0:T(1,128)S(1)} all-to-all(f32[16,9,1,128]{3,2,1,0:T(1,128)S(1)} %shard_map.87), channel_id=1, replica_groups=mesh['z'=16,'core'=2,'state'=16] {'z'}, dimensions={0} | all-to-all | bytes 147456 | tf_op jit(solution)/shard_map/all_to_all | solution.py:296
  89.6 0.1 shard_map.88
  89.7 15.4 %all_to_all.29 = f32[16,8,128]{2,1,0:T(8,128)S(1)} all-to-all(f32[16,8,128]{2,1,0:T(8,128)S(1)} %shard_map.88), channel_id=1, replica_groups=mesh['z'=16,'core'=2,'state'=16] {'z'}, dimensions={0} | all-to-all | bytes 131072 | tf_op jit(solution)/shard_map/all_to_all | solution.py:296
  105.1 4.0 %all-gather.2 = f32[32,8,128]{2,1,0:T(8,128)S(1)} all-gather(f32[16,8,128]{2,1,0:T(8,128)S(1)} %all_to_all.29), channel_id=4, replica_groups=mesh['z'=16,'core'=2,'state'=16] {'core'}, dimensions={0}, use_global_device_ids=true | all-gather | bytes 196608 | tf_op jit(solution)/shard_map/all_gather | solution.py:300
  109.0 0.7 copy.10
  (2 shorter events, 0.0 us)
Async XLA Ops:
  0.0 20.1 %copy-start.4 = (s32[32]{0:T(128)S(1)}, s32[32]{0:T(128)}, u32[]{:S(2)}) copy-start(s32[32]{0:T(128)} %cols_hbm.7) | copy-start | bytes 388
  0.0 20.1 %copy-start.5 = (s32[32]{0:T(128)S(1)}, s32[32]{0:T(128)}, u32[]{:S(2)}) copy-start(s32[32]{0:T(128)} %rows_hbm.5) | copy-start | bytes 388
  0.0 20.1 %copy-start.6 = (f32[16]{0:T(128)S(1)}, f32[16]{0:T(128)}, u32[]{:S(2)}) copy-start(f32[16]{0:T(128)} %betas_hbm.3) | copy-start | bytes 196
  0.0 20.1 %copy-start = (f32[32,64,256]{2,1,0:T(8,128)S(1)}, f32[32,64,256]{2,1,0:T(8,128)}, u32[]{:S(2)}) copy-start(f32[32,64,256]{2,1,0:T(8,128)} %energies_ref.1) | copy-start | bytes 6291460
  0.0 20.1 %copy-start.2 = (s32[1024]{0:T(1024)S(1)}, s32[1024]{0:T(1024)}, u32[]{:S(2)}) copy-start(s32[1024]{0:T(1024)} %param.12) | copy-start | bytes 12292
  3.1 51.4 %copy-start.3 = (s32[1024]{0:T(1024)S(1)}, s32[1024]{0:T(1024)}, u32[]{:S(2)}) copy-start(s32[1024]{0:T(1024)} %param.14) | copy-start | bytes 12292
  22.7 44.9 %copy-start.1 = (bf16[32,16384]{1,0:T(8,128)(2,1)S(1)}, bf16[32,16384]{1,0:T(8,128)(2,1)}, u32[]{:S(2)}) copy-start(bf16[32,16384]{1,0:T(8,128)(2,1)} %basis_ref.1) | copy-start | bytes 3145732

commit v5 on v4

--- a/solution.py
+++ b/solution.py
@@ -38,8 +38,8 @@
 
 def state_beta(temps, betas_ref):
     beta = jnp.zeros(temps.shape, F32)
-    for i in range(betas_ref.shape[0]):
-        beta = jnp.where(temps == i, betas_ref[i], beta)
+    for i in range(betas_ref.shape[-1]):
+        beta = jnp.where(temps == i, betas_ref[:, i:i + 1] if len(betas_ref.shape) == 2 else betas_ref[i], beta)
     return -LOG2E * beta
 
 
@@ -133,14 +133,11 @@
         out_ref[i, cut * slots:] = jnp.broadcast_to(places, (8, LANES))
 
 
-def first_states(rows_hbm, cols_hbm, betas_hbm, temps_ref, energies_ref, parts_ref, out_ref, values_ref, hot_ref,
-                 rows_ref, cols_ref, sems, betas_ref, beta_cols, drop, top, total):
-    index = [
-        pltpu.make_async_copy(rows_hbm, rows_ref, sems.at[0]), pltpu.make_async_copy(cols_hbm, cols_ref, sems.at[1]),
-        pltpu.make_async_copy(betas_hbm, betas_ref, sems.at[2]),
-    ]
-    for copy in index:
-        copy.start()
+def first_states(rows_ref, cols_ref, betas_ref, temps_ref, energies_ref, parts_ref, out_ref, values_ref, hot_ref,
+                 beta_cols, drop, top, total):
+    rows, cols = rows_ref[...], cols_ref[...]
+    rows = [rows[0, t] for t in range(energies_ref.shape[0])]
+    cols = [cols[0, t] for t in range(energies_ref.shape[0])]
     blocks = beta_cols.shape[0] - 1
     slots = energies_ref.shape[0]
     cut = energies_ref.shape[2] // LANES
@@ -169,12 +166,10 @@
         drop[h * blocks_samp:(h + 1) * blocks_samp] = whole[:, h * LANES:(h + 1) * LANES]
     top[...] = jnp.full(top.shape, NEG, F32)
     total[...] = jnp.zeros(total.shape, F32)
-    for copy in index:
-        copy.wait()
     expand(state_beta(temps_ref[...], betas_ref), beta_cols, 0.0)
 
     for t in range(slots):
-        row, col = rows_ref[t], cols_ref[t]
+        row, col = rows[t], cols[t]
         beta = beta_cols[col]
         most = top[col]
         for h, energy in enumerate(halves(energies_ref, t)):
@@ -182,44 +177,35 @@
             values_ref[t, :, h * LANES:(h + 1) * LANES] = value
             most = jnp.maximum(most, value)
         top[col] = most
-    for c in range(blocks):
-        top[c] = jnp.broadcast_to(jnp.max(top[c], axis=1, keepdims=True), top.shape[1:])
-    for t in range(slots):
-        col = cols_ref[t]
+    for t in range(slots):
+        col = cols[t]
         most = top[col]
         part = total[col]
         for value in halves(values_ref, t):
             part = part + jnp.exp2(value - most)
         total[col] = part
     each = LANES // top.shape[1]
-    lane = lax.broadcasted_iota(jnp.int32, (LANES, LANES), 1)
-    tops = jnp.zeros((LANES, LANES), F32)
-    sums = jnp.ones((LANES, LANES), F32)
     for j in range(blocks // each):
         column = range(each * j, each * j + each)
-        tops = jnp.where(lane == j, jnp.concatenate([top[c] for c in column], axis=0), tops)
-        sums = jnp.where(
-            lane == j,
-            jnp.concatenate([jnp.sum(total[c], axis=1, keepdims=True) for c in column], axis=0),
-            sums,
-        )
-    rows = blocks // each
-    out_ref[...] = tops.T[:rows] + jnp.log2(jnp.maximum(sums.T[:rows], 1.0))
+        tops = jnp.concatenate([top[c] for c in column], axis=0).T
+        sums = jnp.concatenate([total[c] for c in column], axis=0).T
+        peak = jnp.max(tops, axis=0, keepdims=True)
+        whole = jnp.sum(sums * jnp.exp2(tops - peak), axis=0, keepdims=True)
+        out_ref[j:j + 1] = peak + jnp.log2(jnp.maximum(whole, 1.0))
 
 
 def both_cores(parts_ref, out_ref):
     copies(out_ref, log_sum(parts_ref[...]))
 
 
-def second_samples(cols_hbm, values_ref, counts_ref, parts_ref, out_ref, weights_ref,
-                   cols_ref, sem, bias_cols, slot):
-    copy = pltpu.make_async_copy(cols_hbm, cols_ref, sem)
-    copy.start()
+def second_samples(cols_ref, values_ref, counts_ref, parts_ref, out_ref, weights_ref,
+                   bias_cols, slot):
+    cols = cols_ref[...]
+    cols = [cols[0, t] for t in range(values_ref.shape[0])]
     slots = values_ref.shape[0]
     expand(log_count(counts_ref) - log_sum(parts_ref[...]), bias_cols, NEG)
-    copy.wait()
-    for t in range(slots):
-        bias = bias_cols[cols_ref[t]]
+    for t in range(slots):
+        bias = bias_cols[cols[t]]
         for h, value in enumerate(halves(values_ref, t)):
             part = jnp.exp2(bias + value)
             weights_ref[t, :, h * LANES:(h + 1) * LANES] = part
@@ -229,13 +215,10 @@
     copies(out_ref, slot[...])
 
 
-def second_states(rows_hbm, cols_hbm, weights_ref, hot_ref, parts_ref, basis_ref, out_ref,
-                  rows_ref, cols_ref, sems, scale, sums):
-    index = [
-        pltpu.make_async_copy(rows_hbm, rows_ref, sems.at[0]), pltpu.make_async_copy(cols_hbm, cols_ref, sems.at[1])
-    ]
-    for copy in index:
-        copy.start()
+def second_states(rows_ref, cols_ref, weights_ref, hot_ref, parts_ref, basis_ref, out_ref, scale, sums):
+    rows, cols = rows_ref[...], cols_ref[...]
+    rows = [rows[0, t] for t in range(weights_ref.shape[0])]
+    cols = [cols[0, t] for t in range(weights_ref.shape[0])]
     blocks = sums.shape[0] - 1
     slots = weights_ref.shape[0]
     count = basis_ref.shape[0]
@@ -248,10 +231,8 @@
         scale[h * blocks_samp:(h + 1) * blocks_samp] = whole[:, h * LANES:(h + 1) * LANES]
     sums[...] = jnp.zeros(sums.shape, F32)
     ones = jnp.ones((sums.shape[1] - count, width), BF16)
-    for copy in index:
-        copy.wait()
-    for t in range(slots):
-        row, col = rows_ref[t], cols_ref[t]
+    for t in range(slots):
+        row, col = rows[t], cols[t]
         weight = jnp.concatenate(
             [part * scale[pl.ds(h * blocks_samp + row, 1)] for h, part in enumerate(halves(weights_ref, t))], axis=1
         )
@@ -350,30 +331,30 @@
             shape(rows, LANES), shape(*energies.shape),
             jax.ShapeDtypeStruct((blocks_samp, n_state * slots), BF16),
         ),
-        anywhere(3) + vmem(3),
-        place + [
-            pltpu.SMEM(betas.shape, F32), pltpu.VMEM(by_state, F32), pltpu.VMEM((cut * blocks_samp, LANES), F32),
+        vmem(6),
+        [
+            pltpu.VMEM(by_state, F32), pltpu.VMEM((cut * blocks_samp, LANES), F32),
             pltpu.VMEM(by_state, F32), pltpu.VMEM(by_state, F32),
         ],
-    )(tile_rows, tile_cols, betas, temps, energies, parts)
+    )(tile_rows.reshape(1, slots), tile_cols.reshape(1, slots), betas.reshape(1, -1), temps, energies, parts)
     parts = pair(parts)
     parts = call(both_cores, shape(n_z, rows, LANES), vmem(1))(parts)
     parts = spread(parts, "z")
     parts, weights = call(
         second_samples,
         (shape(n_state, cut * slots, LANES), shape(*energies.shape)),
-        anywhere(1) + vmem(3),
-        [place[1], pltpu.SemaphoreType.DMA, pltpu.VMEM(by_state, F32), by_slot],
-    )(tile_cols, values, counts, parts)
+        vmem(4),
+        [pltpu.VMEM(by_state, F32), by_slot],
+    )(tile_cols.reshape(1, slots), values, counts, parts)
     parts = spread(parts, "state")
     parts = call(
         second_states,
         shape(n_core, n_z * 9, LANES),
-        anywhere(2) + vmem(4),
-        place + [
+        vmem(6),
+        [
             pltpu.VMEM((cut * blocks_samp, LANES), F32), pltpu.VMEM((blocks + 1, count + 16, state_block), F32)
         ],
-    )(tile_rows, tile_cols, weights, hot, parts, basis)
+    )(tile_rows.reshape(1, slots), tile_cols.reshape(1, slots), weights, hot, parts, basis)
     parts = pair(parts)
     parts = call(core_sums, shape(n_z, 9, 1, LANES), vmem(1))(parts)
     parts = spread(parts, "z")

time: 110 us -> 109 us (level)
  no operation moved by 1% of the time
where the time goes in v5:
time: 109 us
  blocking collectives  101 us (93%)
  Pallas kernels  7.31 us (7%)
    all_to_all x5, blocking collectives, spread(): return lax.all_to_all(parts, axis, 0, 0)  86.4 us
    all_gather x3, blocking collectives, pair(): return lax.all_gather(parts, 'core')  14.3 us
    pallas_call x1, Pallas kernels, on_device(): call(first_samples, shape(n_state, cut * slots + 8, LANES), hbm(7), place...  2.99 us

profile of v5, /device:TPU:1, one launch (start us, length us, event | category | flops | bytes accessed | tf_op | source)
XLA Modules:
  0.0 108.7 jit_solution(11009949769756231417)
XLA Ops:
  0.0 0.0 copy-start.6
  0.0 0.0 copy-start.4
  0.0 0.0 copy-start.5
  0.0 0.0 copy-start
  0.0 0.0 copy-start.2
  0.0 3.0 %shard_map.82 = f32[16,72,128]{2,1,0:T(8,128)} custom-call(s32[32]{0:T(128)} %rows_hbm.1, s32[32]{0:T(128)} %cols_hbm.1, f32[16]{0:T(128)} %betas_hbm.1, f32[32,64,256]{2,1,0:T(8,128)} %energies_ref.1, f32[8,128]{1,0:T(8,128)} %bitcast.26, s32[8,128]{1,0:T(8,128)} %bitcast.15, s32[8,128]{1,0:T(8,128)} %bitcast.17), custom_call_target="tpu_custom_call" | custom-call | tf_op jit(solution)/shard_map/pallas_call | solution.py:315
  3.0 0.0 copy-start.3
  3.0 17.0 %all_to_all.25.parts_ref = f32[16,72,128]{2,1,0:T(8,128)S(1)} all-to-all(f32[16,72,128]{2,1,0:T(8,128)} %shard_map.82), channel_id=1, replica_groups=mesh['z'=16,'core'=2,'state'=16] {'state'}, dimensions={0} | all-to-all | bytes 1179648 | tf_op jit(solution)/shard_map/all_to_all | solution.py:277
  20.1 0.0 copy-done.6
  20.1 0.0 copy-done.4
  20.1 0.0 copy-done.5
  20.1 0.0 copy-done
  20.1 0.0 copy-done.2
  20.1 2.1 %shard_map.83 = (f32[8,128]{1,0:T(8,128)S(1)}, f32[32,64,256]{2,1,0:T(8,128)S(1)}, bf16[64,512]{1,0:T(8,128)(2,1)S(1)}) custom-call(s32[1,32]{1,0:T(1,128)S(1)} %bitcast.22, s32[1,32]{1,0:T(1,128)S(1)} %bitcast.19, f32[1,16]{1,0:T(1,128)S(1)} %bitcast.24, s32[8,128]{1,0:T(8,128)S(1)} %bitcast.16, f32[32,64,256]{2,1,0:T(8,128)S(1)} %copy-done, ...), custom_call_target="tpu_custom_call" | custom-call | tf_op jit(solution)/shard_map/pallas_call | solution.py:328
  22.2 0.0 copy-start.1
  22.2 5.4 %all-gather = f32[16,128]{1,0:T(8,128)S(1)} all-gather(f32[8,128]{1,0:T(8,128)S(1)} %get-tuple-element.11), channel_id=2, replica_groups=mesh['z'=16,'core'=2,'state'=16] {'core'}, dimensions={0}, use_global_device_ids=true | all-gather | bytes 12288 | tf_op jit(solution)/shard_map/all_gather | solution.py:281
  27.7 26.3 %all_to_all.26.parts_ref = f32[16,8,128]{2,1,0:T(8,128)S(1)} all-to-all(f32[16,8,128]{2,1,0:T(8,128)S(1)} %shard_map.84), channel_id=1, replica_groups=mesh['z'=16,'core'=2,'state'=16] {'z'}, dimensions={0} | all-to-all | bytes 131072 | tf_op jit(solution)/shard_map/all_to_all | solution.py:277
  54.0 0.0 copy-done.3
  54.0 0.8 shard_map.85
  54.7 12.2 %all_to_all.27.parts_ref = f32[16,64,128]{2,1,0:T(8,128)S(1)} all-to-all(f32[16,64,128]{2,1,0:T(8,128)S(1)} %get-tuple-element.14), channel_id=1, replica_groups=mesh['z'=16,'core'=2,'state'=16] {'state'}, dimensions={0} | all-to-all | bytes 1048576 | tf_op jit(solution)/shard_map/all_to_all | solution.py:277
  66.9 0.0 copy-done.1
  66.9 1.4 %shard_map.86 = f32[2,144,128]{2,1,0:T(8,128)S(1)} custom-call(s32[1,32]{1,0:T(1,128)S(1)} %bitcast.23, s32[1,32]{1,0:T(1,128)S(1)} %bitcast.21, f32[32,64,256]{2,1,0:T(8,128)S(1)} %get-tuple-element.12.weights_ref, bf16[64,512]{1,0:T(8,128)(2,1)S(1)} %get-tuple-element.13.hot_ref, f32[16,64,128]{2,1,0:T(8,128)S(1)} %all_to_all.27.parts_ref, ...), custom_call_target="tpu_custom_call" | custom-call | tf_op jit(solution)/shard_map/pallas_call | solution.py:350
  68.3 4.9 %all-gather.1 = f32[4,144,128]{2,1,0:T(8,128)S(1)} all-gather(f32[2,144,128]{2,1,0:T(8,128)S(1)} %shard_map.86), channel_id=3, replica_groups=mesh['z'=16,'core'=2,'state'=16] {'core'}, dimensions={0}, use_global_device_ids=true | all-gather | bytes 442368 | tf_op jit(solution)/shard_map/all_gather | solution.py:281
  73.2 15.4 %all_to_all.28.parts_ref = f32[16,9,1,128]{3,2,1,0:T(1,128)S(1)} all-to-all(f32[16,9,1,128]{3,2,1,0:T(1,128)S(1)} %shard_map.87), channel_id=1, replica_groups=mesh['z'=16,'core'=2,'state'=16] {'z'}, dimensions={0} | all-to-all | bytes 147456 | tf_op jit(solution)/shard_map/all_to_all | solution.py:277
  88.7 0.1 shard_map.88
  88.7 15.4 %all_to_all.29 = f32[16,8,128]{2,1,0:T(8,128)S(1)} all-to-all(f32[16,8,128]{2,1,0:T(8,128)S(1)} %shard_map.88), channel_id=1, replica_groups=mesh['z'=16,'core'=2,'state'=16] {'z'}, dimensions={0} | all-to-all | bytes 131072 | tf_op jit(solution)/shard_map/all_to_all | solution.py:277
  104.1 4.0 %all-gather.2 = f32[32,8,128]{2,1,0:T(8,128)S(1)} all-gather(f32[16,8,128]{2,1,0:T(8,128)S(1)} %all_to_all.29), channel_id=4, replica_groups=mesh['z'=16,'core'=2,'state'=16] {'core'}, dimensions={0}, use_global_device_ids=true | all-gather | bytes 196608 | tf_op jit(solution)/shard_map/all_gather | solution.py:281
  108.1 0.7 copy.10
  (2 shorter events, 0.0 us)
Async XLA Ops:
  0.0 20.1 %copy-start.6 = (f32[16]{0:T(128)S(1)}, f32[16]{0:T(128)}, u32[]{:S(2)}) copy-start(f32[16]{0:T(128)} %betas_hbm.1) | copy-start | bytes 196
  0.0 20.1 %copy-start.4 = (s32[32]{0:T(128)S(1)}, s32[32]{0:T(128)}, u32[]{:S(2)}) copy-start(s32[32]{0:T(128)} %cols_hbm.1) | copy-start | bytes 388
  0.0 20.1 %copy-start.5 = (s32[32]{0:T(128)S(1)}, s32[32]{0:T(128)}, u32[]{:S(2)}) copy-start(s32[32]{0:T(128)} %rows_hbm.1) | copy-start | bytes 388
  0.0 20.1 %copy-start = (f32[32,64,256]{2,1,0:T(8,128)S(1)}, f32[32,64,256]{2,1,0:T(8,128)}, u32[]{:S(2)}) copy-start(f32[32,64,256]{2,1,0:T(8,128)} %energies_ref.1) | copy-start | bytes 6291460
  0.0 20.1 %copy-start.2 = (s32[1024]{0:T(1024)S(1)}, s32[1024]{0:T(1024)}, u32[]{:S(2)}) copy-start(s32[1024]{0:T(1024)} %param.12) | copy-start | bytes 12292
  3.0 50.9 %copy-start.3 = (s32[1024]{0:T(1024)S(1)}, s32[1024]{0:T(1024)}, u32[]{:S(2)}) copy-start(s32[1024]{0:T(1024)} %param.14) | copy-start | bytes 12292
  22.2 44.7 %copy-start.1 = (bf16[32,16384]{1,0:T(8,128)(2,1)S(1)}, bf16[32,16384]{1,0:T(8,128)(2,1)}, u32[]{:S(2)}) copy-start(bf16[32,16384]{1,0:T(8,128)(2,1)} %basis_ref.1) | copy-start | bytes 3145732

commit v6 on v5

--- a/solution.py
+++ b/solution.py
@@ -128,9 +128,10 @@
                 slot[h * slots + t:h * slots + t + 1] = peak
                 total[h * slots + t:h * slots + t + 1] = jnp.sum(jnp.exp2(score - peak), axis=0, keepdims=True)
     whole = slot[...] + jnp.log2(jnp.maximum(total[...], 1.0))
-    for i in range(out_ref.shape[0]):
-        out_ref[i, :cut * slots] = whole
-        out_ref[i, cut * slots:] = jnp.broadcast_to(places, (8, LANES))
+    each = cut * slots + 1
+    for i in range(out_ref.shape[0] // each):
+        out_ref[i * each:(i + 1) * each - 1] = whole
+        out_ref[(i + 1) * each - 1:(i + 1) * each] = places
 
 
 def first_states(rows_ref, cols_ref, betas_ref, temps_ref, energies_ref, parts_ref, out_ref, values_ref, hot_ref,
@@ -143,10 +144,13 @@
     cut = energies_ref.shape[2] // LANES
     blocks_samp = drop.shape[0] // cut
     wide = []
-    for j in range(parts_ref.shape[0] * slots // LANES):
+    each = cut * slots + 1
+    peers = parts_ref.shape[0] // each
+    for j in range(peers * slots // LANES):
         places = jnp.zeros((1, LANES), F32)
         for i in range(LANES // slots):
-            place = parts_ref[j * (LANES // slots) + i, cut * slots:cut * slots + 1]
+            end = (j * (LANES // slots) + i + 1) * each
+            place = parts_ref[end - 1:end]
             place = jnp.where(lax.broadcasted_iota(jnp.int32, place.shape, 1) < slots, place, 0.0)
             places = places + (pltpu.roll(place, i * slots, 1) if i else place)
         wide.append(places)
@@ -154,7 +158,15 @@
     row = lax.broadcasted_iota(jnp.int32, (blocks_samp, wide.shape[1]), 0).astype(F32)
     hot = jnp.where(row == wide, 1.0, 0.0).astype(BF16)
     hot_ref[...] = hot
-    parts = jnp.concatenate([by_half(parts_ref, h, slots) for h in range(cut)], axis=1)
+    parts = jnp.concatenate(
+        [
+            jnp.concatenate(
+                [parts_ref[i * each + h * slots:i * each + (h + 1) * slots] for i in range(peers)], axis=0
+            )
+            for h in range(cut)
+        ],
+        axis=1,
+    )
     step = jnp.clip(jnp.floor((parts - BASE) * (1.0 / STEP)), 0.0, LAST)
     power = jnp.exp2(BITS * step).astype(BF16)
     found = jnp.maximum(jnp.dot(hot, power, preferred_element_type=F32), 1.0)
@@ -314,7 +326,7 @@
 
     parts = call(
         first_samples,
-        shape(n_state, cut * slots + 8, LANES),
+        shape(n_state * (cut * slots + 1), LANES),
         hbm(7),
         place[:2] + [
             pltpu.SMEM(betas.shape, F32),
@@ -324,7 +336,7 @@
         ],
         FIRST_VMEM,
     )(tile_rows, tile_cols, betas, energies, free, temps, counts)
-    parts = spread(parts, "state")
+    parts = spread(parts.reshape(n_state, cut * slots + 1, 1, LANES), "state").reshape(-1, LANES)
     parts, values, hot = call(
         first_states,
         (

time: 109 us -> 109 us (level)
  no operation moved by 1% of the time
where the time goes in v6:
time: 109 us; the launch traced here: 108 us
  blocking collectives  100 us (92%)
  Pallas kernels  7.34 us (7%)
    all_to_all x5, blocking collectives, spread(): return lax.all_to_all(parts, axis, 0, 0)  85.7 us
    all_gather x3, blocking collectives, pair(): return lax.all_gather(parts, 'core')  14.3 us
    pallas_call x1, Pallas kernels, on_device(): call(first_samples, shape(n_state * (cut * slots + 1), LANES), hbm(7), pl...  3.03 us

profile of v6, /device:TPU:1, one launch (start us, length us, event | category | flops | bytes accessed | tf_op | source)
XLA Modules:
  0.0 108.2 jit_solution(2233861944392415669)
XLA Ops:
  0.0 0.0 copy-start.6
  0.0 0.0 copy-start.4
  0.0 0.0 copy-start.5
  0.0 0.0 copy-start
  0.0 0.0 copy-start.2
  0.0 3.0 %shard_map.82 = f32[1040,128]{1,0:T(8,128)} custom-call(s32[32]{0:T(128)} %rows_hbm.1, s32[32]{0:T(128)} %cols_hbm.1, f32[16]{0:T(128)} %betas_hbm.1, f32[32,64,256]{2,1,0:T(8,128)} %energies_ref.1, f32[8,128]{1,0:T(8,128)} %bitcast.30, s32[8,128]{1,0:T(8,128)} %bitcast.18, s32[8,128]{1,0:T(8,128)} %bitcast.20), custom_call_target="tpu_custom_call" | custom-call | tf_op jit(solution)/shard_map/pallas_call | solution.py:327
  3.1 0.0 copy-start.3
  3.1 16.9 %all_to_all.25 = f32[16,65,1,128]{3,2,1,0:T(1,128)S(1)} all-to-all(f32[16,65,1,128]{3,2,1,0:T(1,128)} %bitcast.28), channel_id=1, replica_groups=mesh['z'=16,'core'=2,'state'=16] {'state'}, dimensions={0} | all-to-all | bytes 1064960 | tf_op jit(solution)/shard_map/all_to_all | solution.py:289
  20.0 0.0 copy-done.6
  20.0 0.0 copy-done.4
  20.0 0.0 copy-done.5
  20.0 0.0 copy-done
  20.0 0.0 copy-done.2
  20.0 2.1 %shard_map.83 = (f32[8,128]{1,0:T(8,128)S(1)}, f32[32,64,256]{2,1,0:T(8,128)S(1)}, bf16[64,512]{1,0:T(8,128)(2,1)S(1)}) custom-call(s32[1,32]{1,0:T(1,128)S(1)} %bitcast.25, s32[1,32]{1,0:T(1,128)S(1)} %bitcast.22, f32[1,16]{1,0:T(1,128)S(1)} %bitcast.27, s32[8,128]{1,0:T(8,128)S(1)} %bitcast.19, f32[32,64,256]{2,1,0:T(8,128)S(1)} %copy-done, ...), custom_call_target="tpu_custom_call" | custom-call | tf_op jit(solution)/shard_map/pallas_call | solution.py:340
  22.1 0.0 copy-start.1
  22.1 5.5 %all-gather = f32[16,128]{1,0:T(8,128)S(1)} all-gather(f32[8,128]{1,0:T(8,128)S(1)} %get-tuple-element.11), channel_id=2, replica_groups=mesh['z'=16,'core'=2,'state'=16] {'core'}, dimensions={0}, use_global_device_ids=true | all-gather | bytes 12288 | tf_op jit(solution)/shard_map/all_gather | solution.py:293
  27.6 26.0 %all_to_all.26.parts_ref = f32[16,8,128]{2,1,0:T(8,128)S(1)} all-to-all(f32[16,8,128]{2,1,0:T(8,128)S(1)} %shard_map.84), channel_id=1, replica_groups=mesh['z'=16,'core'=2,'state'=16] {'z'}, dimensions={0} | all-to-all | bytes 131072 | tf_op jit(solution)/shard_map/all_to_all | solution.py:289
  53.5 0.0 copy-done.3
  53.5 0.8 shard_map.85
  54.3 12.0 %all_to_all.27.parts_ref = f32[16,64,128]{2,1,0:T(8,128)S(1)} all-to-all(f32[16,64,128]{2,1,0:T(8,128)S(1)} %get-tuple-element.14), channel_id=1, replica_groups=mesh['z'=16,'core'=2,'state'=16] {'state'}, dimensions={0} | all-to-all | bytes 1048576 | tf_op jit(solution)/shard_map/all_to_all | solution.py:289
  66.4 0.0 copy-done.1
  66.4 1.4 %shard_map.86 = f32[2,144,128]{2,1,0:T(8,128)S(1)} custom-call(s32[1,32]{1,0:T(1,128)S(1)} %bitcast.26, s32[1,32]{1,0:T(1,128)S(1)} %bitcast.24, f32[32,64,256]{2,1,0:T(8,128)S(1)} %get-tuple-element.12.weights_ref, bf16[64,512]{1,0:T(8,128)(2,1)S(1)} %get-tuple-element.13.hot_ref, f32[16,64,128]{2,1,0:T(8,128)S(1)} %all_to_all.27.parts_ref, ...), custom_call_target="tpu_custom_call" | custom-call | tf_op jit(solution)/shard_map/pallas_call | solution.py:362
  67.8 4.9 %all-gather.1 = f32[4,144,128]{2,1,0:T(8,128)S(1)} all-gather(f32[2,144,128]{2,1,0:T(8,128)S(1)} %shard_map.86), channel_id=3, replica_groups=mesh['z'=16,'core'=2,'state'=16] {'core'}, dimensions={0}, use_global_device_ids=true | all-gather | bytes 442368 | tf_op jit(solution)/shard_map/all_gather | solution.py:293
  72.7 15.4 %all_to_all.28.parts_ref = f32[16,9,1,128]{3,2,1,0:T(1,128)S(1)} all-to-all(f32[16,9,1,128]{3,2,1,0:T(1,128)S(1)} %shard_map.87), channel_id=1, replica_groups=mesh['z'=16,'core'=2,'state'=16] {'z'}, dimensions={0} | all-to-all | bytes 147456 | tf_op jit(solution)/shard_map/all_to_all | solution.py:289
  88.1 0.1 shard_map.88
  88.2 15.4 %all_to_all.29 = f32[16,8,128]{2,1,0:T(8,128)S(1)} all-to-all(f32[16,8,128]{2,1,0:T(8,128)S(1)} %shard_map.88), channel_id=1, replica_groups=mesh['z'=16,'core'=2,'state'=16] {'z'}, dimensions={0} | all-to-all | bytes 131072 | tf_op jit(solution)/shard_map/all_to_all | solution.py:289
  103.6 4.0 %all-gather.2 = f32[32,8,128]{2,1,0:T(8,128)S(1)} all-gather(f32[16,8,128]{2,1,0:T(8,128)S(1)} %all_to_all.29), channel_id=4, replica_groups=mesh['z'=16,'core'=2,'state'=16] {'core'}, dimensions={0}, use_global_device_ids=true | all-gather | bytes 196608 | tf_op jit(solution)/shard_map/all_gather | solution.py:293
  107.5 0.7 copy.11
  (2 shorter events, 0.0 us)
Async XLA Ops:
  0.0 20.0 %copy-start.6 = (f32[16]{0:T(128)S(1)}, f32[16]{0:T(128)}, u32[]{:S(2)}) copy-start(f32[16]{0:T(128)} %betas_hbm.1) | copy-start | bytes 196
  0.0 20.0 %copy-start.4 = (s32[32]{0:T(128)S(1)}, s32[32]{0:T(128)}, u32[]{:S(2)}) copy-start(s32[32]{0:T(128)} %cols_hbm.1) | copy-start | bytes 388
  0.0 20.0 %copy-start.5 = (s32[32]{0:T(128)S(1)}, s32[32]{0:T(128)}, u32[]{:S(2)}) copy-start(s32[32]{0:T(128)} %rows_hbm.1) | copy-start | bytes 388
  0.0 20.0 %copy-start = (f32[32,64,256]{2,1,0:T(8,128)S(1)}, f32[32,64,256]{2,1,0:T(8,128)}, u32[]{:S(2)}) copy-start(f32[32,64,256]{2,1,0:T(8,128)} %energies_ref.1) | copy-start | bytes 6291460
  0.0 20.0 %copy-start.2 = (s32[1024]{0:T(1024)S(1)}, s32[1024]{0:T(1024)}, u32[]{:S(2)}) copy-start(s32[1024]{0:T(1024)} %param.12) | copy-start | bytes 12292
  3.1 50.5 %copy-start.3 = (s32[1024]{0:T(1024)S(1)}, s32[1024]{0:T(1024)}, u32[]{:S(2)}) copy-start(s32[1024]{0:T(1024)} %param.14) | copy-start | bytes 12292
  22.1 44.3 %copy-start.1 = (bf16[32,16384]{1,0:T(8,128)(2,1)S(1)}, bf16[32,16384]{1,0:T(8,128)(2,1)}, u32[]{:S(2)}) copy-start(bf16[32,16384]{1,0:T(8,128)(2,1)} %basis_ref.1) | copy-start | bytes 3145732

commit v7 on v6

--- a/solution.py
+++ b/solution.py
@@ -8,7 +8,7 @@
 NEG = -1e30
 TINY = 1e-30
 LANES = 128
-UNROLL = 4
+UNROLL = 8
 MIB = 1024 * 1024
 FIRST_VMEM = 60 * MIB
 F32 = jnp.float32

time: 109 us -> 108 us (level)
  no operation moved by 1% of the time
where the time goes in v7:
time: 108 us
  blocking collectives  100 us (93%)
  Pallas kernels  7.19 us (7%)
    all_to_all x5, blocking collectives, spread(): return lax.all_to_all(parts, axis, 0, 0)  85.7 us
    all_gather x3, blocking collectives, pair(): return lax.all_gather(parts, 'core')  14.4 us
    pallas_call x1, Pallas kernels, on_device(): call(first_samples, shape(n_state * (cut * slots + 1), LANES), hbm(7), pl...  2.9 us

profile of v7, /device:TPU:1, one launch (start us, length us, event | category | flops | bytes accessed | tf_op | source)
XLA Modules:
  0.0 108.0 jit_solution(6676953753720527231)
XLA Ops:
  0.0 0.0 copy-start.6
  0.0 0.0 copy-start.4
  0.0 0.0 copy-start.5
  0.0 0.0 copy-start
  0.0 0.0 copy-start.2
  0.0 2.9 %shard_map.82 = f32[1040,128]{1,0:T(8,128)} custom-call(s32[32]{0:T(128)} %rows_hbm.1, s32[32]{0:T(128)} %cols_hbm.1, f32[16]{0:T(128)} %betas_hbm.1, f32[32,64,256]{2,1,0:T(8,128)} %energies_ref.1, f32[8,128]{1,0:T(8,128)} %bitcast.30, s32[8,128]{1,0:T(8,128)} %bitcast.18, s32[8,128]{1,0:T(8,128)} %bitcast.20), custom_call_target="tpu_custom_call" | custom-call | tf_op jit(solution)/shard_map/pallas_call | solution.py:327
  2.9 0.0 copy-start.3
  3.0 16.9 %all_to_all.25 = f32[16,65,1,128]{3,2,1,0:T(1,128)S(1)} all-to-all(f32[16,65,1,128]{3,2,1,0:T(1,128)} %bitcast.28), channel_id=1, replica_groups=mesh['z'=16,'core'=2,'state'=16] {'state'}, dimensions={0} | all-to-all | bytes 1064960 | tf_op jit(solution)/shard_map/all_to_all | solution.py:289
  19.8 0.0 copy-done.6
  19.8 0.0 copy-done.4
  19.8 0.0 copy-done.5
  19.8 0.0 copy-done
  19.9 0.0 copy-done.2
  19.9 2.1 %shard_map.83 = (f32[8,128]{1,0:T(8,128)S(1)}, f32[32,64,256]{2,1,0:T(8,128)S(1)}, bf16[64,512]{1,0:T(8,128)(2,1)S(1)}) custom-call(s32[1,32]{1,0:T(1,128)S(1)} %bitcast.25, s32[1,32]{1,0:T(1,128)S(1)} %bitcast.22, f32[1,16]{1,0:T(1,128)S(1)} %bitcast.27, s32[8,128]{1,0:T(8,128)S(1)} %bitcast.19, f32[32,64,256]{2,1,0:T(8,128)S(1)} %copy-done, ...), custom_call_target="tpu_custom_call" | custom-call | tf_op jit(solution)/shard_map/pallas_call | solution.py:340
  21.9 0.0 copy-start.1
  21.9 5.5 %all-gather = f32[16,128]{1,0:T(8,128)S(1)} all-gather(f32[8,128]{1,0:T(8,128)S(1)} %get-tuple-element.11), channel_id=2, replica_groups=mesh['z'=16,'core'=2,'state'=16] {'core'}, dimensions={0}, use_global_device_ids=true | all-gather | bytes 12288 | tf_op jit(solution)/shard_map/all_gather | solution.py:293
  27.4 26.0 %all_to_all.26.parts_ref = f32[16,8,128]{2,1,0:T(8,128)S(1)} all-to-all(f32[16,8,128]{2,1,0:T(8,128)S(1)} %shard_map.84), channel_id=1, replica_groups=mesh['z'=16,'core'=2,'state'=16] {'z'}, dimensions={0} | all-to-all | bytes 131072 | tf_op jit(solution)/shard_map/all_to_all | solution.py:289
  53.4 0.0 copy-done.3
  53.4 0.8 shard_map.85
  54.2 12.0 %all_to_all.27.parts_ref = f32[16,64,128]{2,1,0:T(8,128)S(1)} all-to-all(f32[16,64,128]{2,1,0:T(8,128)S(1)} %get-tuple-element.14), channel_id=1, replica_groups=mesh['z'=16,'core'=2,'state'=16] {'state'}, dimensions={0} | all-to-all | bytes 1048576 | tf_op jit(solution)/shard_map/all_to_all | solution.py:289
  66.2 0.0 copy-done.1
  66.2 1.4 %shard_map.86 = f32[2,144,128]{2,1,0:T(8,128)S(1)} custom-call(s32[1,32]{1,0:T(1,128)S(1)} %bitcast.26, s32[1,32]{1,0:T(1,128)S(1)} %bitcast.24, f32[32,64,256]{2,1,0:T(8,128)S(1)} %get-tuple-element.12.weights_ref, bf16[64,512]{1,0:T(8,128)(2,1)S(1)} %get-tuple-element.13.hot_ref, f32[16,64,128]{2,1,0:T(8,128)S(1)} %all_to_all.27.parts_ref, ...), custom_call_target="tpu_custom_call" | custom-call | tf_op jit(solution)/shard_map/pallas_call | solution.py:362
  67.6 4.9 %all-gather.1 = f32[4,144,128]{2,1,0:T(8,128)S(1)} all-gather(f32[2,144,128]{2,1,0:T(8,128)S(1)} %shard_map.86), channel_id=3, replica_groups=mesh['z'=16,'core'=2,'state'=16] {'core'}, dimensions={0}, use_global_device_ids=true | all-gather | bytes 442368 | tf_op jit(solution)/shard_map/all_gather | solution.py:293
  72.5 15.4 %all_to_all.28.parts_ref = f32[16,9,1,128]{3,2,1,0:T(1,128)S(1)} all-to-all(f32[16,9,1,128]{3,2,1,0:T(1,128)S(1)} %shard_map.87), channel_id=1, replica_groups=mesh['z'=16,'core'=2,'state'=16] {'z'}, dimensions={0} | all-to-all | bytes 147456 | tf_op jit(solution)/shard_map/all_to_all | solution.py:289
  87.9 0.1 shard_map.88
  88.0 15.4 %all_to_all.29 = f32[16,8,128]{2,1,0:T(8,128)S(1)} all-to-all(f32[16,8,128]{2,1,0:T(8,128)S(1)} %shard_map.88), channel_id=1, replica_groups=mesh['z'=16,'core'=2,'state'=16] {'z'}, dimensions={0} | all-to-all | bytes 131072 | tf_op jit(solution)/shard_map/all_to_all | solution.py:289
  103.4 4.0 %all-gather.2 = f32[32,8,128]{2,1,0:T(8,128)S(1)} all-gather(f32[16,8,128]{2,1,0:T(8,128)S(1)} %all_to_all.29), channel_id=4, replica_groups=mesh['z'=16,'core'=2,'state'=16] {'core'}, dimensions={0}, use_global_device_ids=true | all-gather | bytes 196608 | tf_op jit(solution)/shard_map/all_gather | solution.py:293
  107.4 0.7 copy.11
  (2 shorter events, 0.0 us)
Async XLA Ops:
  0.0 19.8 %copy-start.6 = (f32[16]{0:T(128)S(1)}, f32[16]{0:T(128)}, u32[]{:S(2)}) copy-start(f32[16]{0:T(128)} %betas_hbm.1) | copy-start | bytes 196
  0.0 19.8 %copy-start.4 = (s32[32]{0:T(128)S(1)}, s32[32]{0:T(128)}, u32[]{:S(2)}) copy-start(s32[32]{0:T(128)} %cols_hbm.1) | copy-start | bytes 388
  0.0 19.8 %copy-start.5 = (s32[32]{0:T(128)S(1)}, s32[32]{0:T(128)}, u32[]{:S(2)}) copy-start(s32[32]{0:T(128)} %rows_hbm.1) | copy-start | bytes 388
  0.0 19.8 %copy-start = (f32[32,64,256]{2,1,0:T(8,128)S(1)}, f32[32,64,256]{2,1,0:T(8,128)}, u32[]{:S(2)}) copy-start(f32[32,64,256]{2,1,0:T(8,128)} %energies_ref.1) | copy-start | bytes 6291460
  0.0 19.8 %copy-start.2 = (s32[1024]{0:T(1024)S(1)}, s32[1024]{0:T(1024)}, u32[]{:S(2)}) copy-start(s32[1024]{0:T(1024)} %param.12) | copy-start | bytes 12292
  2.9 50.5 %copy-start.3 = (s32[1024]{0:T(1024)S(1)}, s32[1024]{0:T(1024)}, u32[]{:S(2)}) copy-start(s32[1024]{0:T(1024)} %param.14) | copy-start | bytes 12292
  21.9 44.3 %copy-start.1 = (bf16[32,16384]{1,0:T(8,128)(2,1)S(1)}, bf16[32,16384]{1,0:T(8,128)(2,1)}, u32[]{:S(2)}) copy-start(bf16[32,16384]{1,0:T(8,128)(2,1)} %basis_ref.1) | copy-start | bytes 3145732

commit v8 on v7

--- a/solution.py
+++ b/solution.py
@@ -8,9 +8,8 @@
 NEG = -1e30
 TINY = 1e-30
 LANES = 128
-UNROLL = 8
 MIB = 1024 * 1024
-FIRST_VMEM = 60 * MIB
+COST = 10**10
 F32 = jnp.float32
 BF16 = jnp.bfloat16
 LOG2E = 1.4426950408889634
@@ -24,22 +23,10 @@
     return [pl.BlockSpec(memory_space=pltpu.VMEM)] * count
 
 
-def smem(count):
-    return [pl.BlockSpec(memory_space=pltpu.SMEM)] * count
-
-
-def hbm(count):
-    return [pl.BlockSpec(memory_space=pltpu.HBM)] * count
-
-
-def anywhere(count):
-    return [pl.BlockSpec(memory_space=pl.ANY)] * count
-
-
 def state_beta(temps, betas_ref):
     beta = jnp.zeros(temps.shape, F32)
     for i in range(betas_ref.shape[-1]):
-        beta = jnp.where(temps == i, betas_ref[:, i:i + 1] if len(betas_ref.shape) == 2 else betas_ref[i], beta)
+        beta = jnp.where(temps == i, betas_ref[:, i:i + 1], beta)
     return -LOG2E * beta
 
 
@@ -88,45 +75,28 @@
     return values.reshape(values.shape[0] * slots, LANES)
 
 
-def first_samples(rows_hbm, cols_hbm, betas_hbm, energies_hbm, free_hbm, temps_hbm, counts_hbm,
-                  out_ref,
-                  rows_ref, cols_ref, betas_ref, energies_ref, free_ref, temps_ref, counts_ref,
-                  beta_cols, bias_cols, slot, total, sems):
+def begin(out_ref):
+    out_ref[...] = jnp.zeros(out_ref.shape, F32)
+
+
+def state_columns(betas_ref, free_ref, temps_ref, counts_ref, start_ref, beta_cols, bias_cols):
+    expand(state_beta(temps_ref[...], betas_ref), beta_cols, 0.0)
+    expand(log_count(counts_ref) + LOG2E * free_ref[...] + start_ref[...], bias_cols, NEG)
+
+
+def first_samples(rows_ref, cols_ref, beta_cols, bias_cols, energies_ref, out_ref, slot, total):
     slots = energies_ref.shape[0]
     cut = energies_ref.shape[2] // LANES
-    small = [
-        pltpu.make_async_copy(source, target, sems.at[i])
-        for i, (source, target) in enumerate([
-            (temps_hbm, temps_ref), (counts_hbm, counts_ref), (free_hbm, free_ref),
-            (betas_hbm, betas_ref), (cols_hbm, cols_ref), (rows_hbm, rows_ref),
-        ])
-    ]
-    large = [
-        pltpu.make_async_copy(
-            energies_hbm.at[pl.ds(g * UNROLL, UNROLL)], energies_ref.at[pl.ds(g * UNROLL, UNROLL)],
-            sems.at[len(small) + g],
-        )
-        for g in range(slots // UNROLL)
-    ]
-    for copy in small + large:
-        copy.start()
-    for copy in small:
-        copy.wait()
-    expand(state_beta(temps_ref[...], betas_ref), beta_cols, 0.0)
-    expand(log_count(counts_ref) + LOG2E * free_ref[...], bias_cols, NEG)
-    lane = lax.broadcasted_iota(jnp.int32, (1, LANES), 1)
-    places = jnp.zeros((1, LANES), F32)
-    for t in range(slots):
-        places = jnp.where(lane == t, rows_ref[t].astype(F32), places)
-    for g in range(slots // UNROLL):
-        large[g].wait()
-        for t in range(g * UNROLL, (g + 1) * UNROLL):
-            beta, bias = beta_cols[cols_ref[t]], bias_cols[cols_ref[t]]
-            for h, energy in enumerate(halves(energies_ref, t)):
-                score = bias + beta * energy
-                peak = jnp.max(score, axis=0, keepdims=True)
-                slot[h * slots + t:h * slots + t + 1] = peak
-                total[h * slots + t:h * slots + t + 1] = jnp.sum(jnp.exp2(score - peak), axis=0, keepdims=True)
+    rows, cols = rows_ref[...], cols_ref[...]
+    cols = [cols[0, t] for t in range(slots)]
+    places = jnp.concatenate([rows.astype(F32), jnp.zeros((1, LANES - slots), F32)], axis=1)
+    for t in range(slots):
+        beta, bias = beta_cols[cols[t]], bias_cols[cols[t]]
+        for h, energy in enumerate(halves(energies_ref, t)):
+            score = bias + beta * energy
+            peak = jnp.max(score, axis=0, keepdims=True)
+            slot[h * slots + t:h * slots + t + 1] = peak
+            total[h * slots + t:h * slots + t + 1] = jnp.sum(jnp.exp2(score - peak), axis=0, keepdims=True)
     whole = slot[...] + jnp.log2(jnp.maximum(total[...], 1.0))
     each = cut * slots + 1
     for i in range(out_ref.shape[0] // each):
@@ -134,8 +104,8 @@
         out_ref[(i + 1) * each - 1:(i + 1) * each] = places
 
 
-def first_states(rows_ref, cols_ref, betas_ref, temps_ref, energies_ref, parts_ref, out_ref, values_ref, hot_ref,
-                 beta_cols, drop, top, total):
+def first_states(rows_ref, cols_ref, beta_cols, energies_ref, parts_ref, out_ref, values_ref, hot_ref,
+                 drop, top, total):
     rows, cols = rows_ref[...], cols_ref[...]
     rows = [rows[0, t] for t in range(energies_ref.shape[0])]
     cols = [cols[0, t] for t in range(energies_ref.shape[0])]
@@ -178,7 +148,6 @@
         drop[h * blocks_samp:(h + 1) * blocks_samp] = whole[:, h * LANES:(h + 1) * LANES]
     top[...] = jnp.full(top.shape, NEG, F32)
     total[...] = jnp.zeros(total.shape, F32)
-    expand(state_beta(temps_ref[...], betas_ref), beta_cols, 0.0)
 
     for t in range(slots):
         row, col = rows[t], cols[t]
@@ -293,7 +262,7 @@
     return lax.all_gather(parts, "core")
 
 
-def call(kernel, out_shape, in_specs, scratch_shapes=(), limit=40 * MIB):
+def call(kernel, out_shape, in_specs, scratch_shapes=(), cost=None):
     single = not isinstance(out_shape, tuple)
     return pl.pallas_call(
         kernel,
@@ -301,7 +270,8 @@
         in_specs=in_specs,
         out_specs=vmem(1)[0] if single else tuple(vmem(len(out_shape))),
         scratch_shapes=list(scratch_shapes),
-        compiler_params=pltpu.CompilerParams(vmem_limit_bytes=limit),
+        compiler_params=pltpu.CompilerParams(vmem_limit_bytes=40 * MIB),
+        cost_estimate=cost,
     )
 
 
@@ -315,27 +285,15 @@
     count = basis.shape[0]
     shape = lambda *dims: jax.ShapeDtypeStruct(dims, F32)
     by_state = (blocks + 1, state_block, LANES)
-    place = [
-        pltpu.SMEM(tile_rows.shape, jnp.int32), pltpu.SMEM(tile_cols.shape, jnp.int32), pltpu.SemaphoreType.DMA((3,))
-    ]
-    flat = pltpu.VMEM((rows, LANES), F32)
-    whole = pltpu.VMEM((rows, LANES), jnp.int32)
     by_slot = pltpu.VMEM((cut * slots, LANES), F32)
-
     free, temps, counts = (vector.reshape(rows, LANES) for vector in (start_free, temps, counts))
 
-    parts = call(
-        first_samples,
-        shape(n_state * (cut * slots + 1), LANES),
-        hbm(7),
-        place[:2] + [
-            pltpu.SMEM(betas.shape, F32),
-            pltpu.VMEM(energies.shape, F32),
-            flat, whole, whole, pltpu.VMEM(by_state, F32), pltpu.VMEM(by_state, F32), by_slot, by_slot,
-            pltpu.SemaphoreType.DMA((6 + slots // UNROLL,)),
-        ],
-        FIRST_VMEM,
-    )(tile_rows, tile_cols, betas, energies, free, temps, counts)
+    tile_rows, tile_cols, betas = (vector.reshape(1, -1) for vector in (tile_rows, tile_cols, betas))
+    start = call(begin, shape(rows, LANES), [], cost=pl.CostEstimate(flops=COST, bytes_accessed=0, transcendentals=0))()
+    beta, bias = call(state_columns, (shape(*by_state), shape(*by_state)), vmem(5))(betas, free, temps, counts, start)
+    parts = call(first_samples, shape(n_state * (cut * slots + 1), LANES), vmem(5), [by_slot, by_slot])(
+        tile_rows, tile_cols, beta, bias, energies
+    )
     parts = spread(parts.reshape(n_state, cut * slots + 1, 1, LANES), "state").reshape(-1, LANES)
     parts, values, hot = call(
         first_states,
@@ -343,12 +301,12 @@
             shape(rows, LANES), shape(*energies.shape),
             jax.ShapeDtypeStruct((blocks_samp, n_state * slots), BF16),
         ),
-        vmem(6),
+        vmem(5),
         [
-            pltpu.VMEM(by_state, F32), pltpu.VMEM((cut * blocks_samp, LANES), F32),
+            pltpu.VMEM((cut * blocks_samp, LANES), F32),
             pltpu.VMEM(by_state, F32), pltpu.VMEM(by_state, F32),
         ],
-    )(tile_rows.reshape(1, slots), tile_cols.reshape(1, slots), betas.reshape(1, -1), temps, energies, parts)
+    )(tile_rows, tile_cols, beta, energies, parts)
     parts = pair(parts)
     parts = call(both_cores, shape(n_z, rows, LANES), vmem(1))(parts)
     parts = spread(parts, "z")
@@ -357,7 +315,7 @@
         (shape(n_state, cut * slots, LANES), shape(*energies.shape)),
         vmem(4),
         [pltpu.VMEM(by_state, F32), by_slot],
-    )(tile_cols.reshape(1, slots), values, counts, parts)
+    )(tile_cols, values, counts, parts)
     parts = spread(parts, "state")
     parts = call(
         second_states,
@@ -366,7 +324,7 @@
         [
             pltpu.VMEM((cut * blocks_samp, LANES), F32), pltpu.VMEM((blocks + 1, count + 16, state_block), F32)
         ],
-    )(tile_rows.reshape(1, slots), tile_cols.reshape(1, slots), weights, hot, parts, basis)
+    )(tile_rows, tile_cols, weights, hot, parts, basis)
     parts = pair(parts)
     parts = call(core_sums, shape(n_z, 9, 1, LANES), vmem(1))(parts)
     parts = spread(parts, "z")

time: 108 us -> 107 us (level)
  Pallas kernels: 7.19 us -> 5.39 us
    pallas_call x1 -> x3, Pallas kernels: 2.9 us -> 1.18 us  [the longest x1 0.64 us: on_device(): call(first_samples, shape(n_state * (cut * slots + 1), LANES), vmem(5), [...]
where the time goes in v8:
time: 107 us
  blocking collectives  99.9 us (93%)
  Pallas kernels  5.39 us (5%)
  local copies, waits for them, and re-layouts  1.73 us (2%)
    all_to_all x5, blocking collectives, spread(): return lax.all_to_all(parts, axis, 0, 0)  86 us
    all_gather x3, blocking collectives, pair(): return lax.all_gather(parts, 'core')  13.8 us

profile of v8, /device:TPU:1, one launch (start us, length us, event | category | flops | bytes accessed | tf_op | source)
XLA Modules:
  0.0 107.1 jit_solution(10765627993278225823)
XLA Ops:
  0.0 0.0 copy-start.2
  0.0 0.0 copy-start.7
  0.0 0.0 copy-start.6
  0.0 0.0 copy-start.5
  0.0 0.0 copy-start
  0.0 0.0 copy-start.3
  0.0 0.0 copy-start.4
  0.1 0.6 copy-done.2
  0.7 0.0 copy-done.7
  0.7 0.0 copy-done.6
  0.7 0.0 copy-done.5
  0.7 0.5 shard_map.83
  1.3 0.4 copy-done
  1.7 0.0 copy-done.3
  1.7 0.0 copy-done.4
  1.7 0.6 shard_map.84
  2.3 16.8 %all_to_all.25 = f32[16,65,1,128]{3,2,1,0:T(1,128)S(1)} all-to-all(f32[16,65,1,128]{3,2,1,0:T(1,128)S(1)} %bitcast.16), channel_id=1, replica_groups=mesh['z'=16,'core'=2,'state'=16] {'state'}, dimensions={0} | all-to-all | bytes 1064960 | tf_op jit(solution)/shard_map/all_to_all | solution.py:258
  19.1 2.0 %shard_map.85 = (f32[8,128]{1,0:T(8,128)S(1)}, f32[32,64,256]{2,1,0:T(8,128)S(1)}, bf16[64,512]{1,0:T(8,128)(2,1)S(1)}) custom-call(s32[1,32]{1,0:T(1,128)S(1)} %bitcast.26, s32[1,32]{1,0:T(1,128)S(1)} %bitcast.22, f32[17,64,128]{2,1,0:T(8,128)S(1)} %get-tuple-element.12.beta_cols, f32[32,64,256]{2,1,0:T(8,128)S(1)} %copy-done, f32[1040,128]{1,0:T(8,128)S(1)} %bitcast.15), custom_call_target="tpu_custom_call" | custom-call | tf_op jit(solution)/shard_map/pallas_call | solution.py:298
  21.1 0.0 copy-start.1
  21.1 5.0 %all-gather = f32[16,128]{1,0:T(8,128)S(1)} all-gather(f32[8,128]{1,0:T(8,128)S(1)} %get-tuple-element.15), channel_id=2, replica_groups=mesh['z'=16,'core'=2,'state'=16] {'core'}, dimensions={0}, use_global_device_ids=true | all-gather | bytes 12288 | tf_op jit(solution)/shard_map/all_gather | solution.py:262
  26.1 26.4 %all_to_all.26.parts_ref = f32[16,8,128]{2,1,0:T(8,128)S(1)} all-to-all(f32[16,8,128]{2,1,0:T(8,128)S(1)} %shard_map.86), channel_id=1, replica_groups=mesh['z'=16,'core'=2,'state'=16] {'z'}, dimensions={0} | all-to-all | bytes 131072 | tf_op jit(solution)/shard_map/all_to_all | solution.py:258
  52.5 0.8 shard_map.87
  53.3 12.0 %all_to_all.27.parts_ref = f32[16,64,128]{2,1,0:T(8,128)S(1)} all-to-all(f32[16,64,128]{2,1,0:T(8,128)S(1)} %get-tuple-element.18), channel_id=1, replica_groups=mesh['z'=16,'core'=2,'state'=16] {'state'}, dimensions={0} | all-to-all | bytes 1048576 | tf_op jit(solution)/shard_map/all_to_all | solution.py:258
  65.3 0.0 copy-done.1
  65.3 1.4 %shard_map.88 = f32[2,144,128]{2,1,0:T(8,128)S(1)} custom-call(s32[1,32]{1,0:T(1,128)S(1)} %bitcast.27, s32[1,32]{1,0:T(1,128)S(1)} %bitcast.24, f32[32,64,256]{2,1,0:T(8,128)S(1)} %get-tuple-element.16.weights_ref, bf16[64,512]{1,0:T(8,128)(2,1)S(1)} %get-tuple-element.17.hot_ref, f32[16,64,128]{2,1,0:T(8,128)S(1)} %all_to_all.27.parts_ref, ...), custom_call_target="tpu_custom_call" | custom-call | tf_op jit(solution)/shard_map/pallas_call | solution.py:320
  66.6 4.9 %all-gather.1 = f32[4,144,128]{2,1,0:T(8,128)S(1)} all-gather(f32[2,144,128]{2,1,0:T(8,128)S(1)} %shard_map.88), channel_id=3, replica_groups=mesh['z'=16,'core'=2,'state'=16] {'core'}, dimensions={0}, use_global_device_ids=true | all-gather | bytes 442368 | tf_op jit(solution)/shard_map/all_gather | solution.py:262
  71.6 15.4 %all_to_all.28.parts_ref = f32[16,9,1,128]{3,2,1,0:T(1,128)S(1)} all-to-all(f32[16,9,1,128]{3,2,1,0:T(1,128)S(1)} %shard_map.89), channel_id=1, replica_groups=mesh['z'=16,'core'=2,'state'=16] {'z'}, dimensions={0} | all-to-all | bytes 147456 | tf_op jit(solution)/shard_map/all_to_all | solution.py:258
  87.0 0.1 shard_map.90
  87.1 15.4 %all_to_all.29 = f32[16,8,128]{2,1,0:T(8,128)S(1)} all-to-all(f32[16,8,128]{2,1,0:T(8,128)S(1)} %shard_map.90), channel_id=1, replica_groups=mesh['z'=16,'core'=2,'state'=16] {'z'}, dimensions={0} | all-to-all | bytes 131072 | tf_op jit(solution)/shard_map/all_to_all | solution.py:258
  102.5 4.0 %all-gather.2 = f32[32,8,128]{2,1,0:T(8,128)S(1)} all-gather(f32[16,8,128]{2,1,0:T(8,128)S(1)} %all_to_all.29), channel_id=4, replica_groups=mesh['z'=16,'core'=2,'state'=16] {'core'}, dimensions={0}, use_global_device_ids=true | all-gather | bytes 196608 | tf_op jit(solution)/shard_map/all_gather | solution.py:262
  106.4 0.7 copy.11
  (3 shorter events, 0.0 us)
Async XLA Ops:
  0.0 0.7 copy-start.2
  0.0 0.7 copy-start.7
  0.0 0.7 copy-start.6
  0.0 0.7 copy-start.5
  0.0 1.6 %copy-start = (f32[32,64,256]{2,1,0:T(8,128)S(1)}, f32[32,64,256]{2,1,0:T(8,128)}, u32[]{:S(2)}) copy-start(f32[32,64,256]{2,1,0:T(8,128)} %energies_ref.3) | copy-start | bytes 6291460
  0.0 1.6 %copy-start.3 = (s32[32]{0:T(128)S(1)}, s32[32]{0:T(128)}, u32[]{:S(2)}) copy-start(s32[32]{0:T(128)} %param.10) | copy-start | bytes 388
  0.0 1.6 %copy-start.4 = (s32[32]{0:T(128)S(1)}, s32[32]{0:T(128)}, u32[]{:S(2)}) copy-start(s32[32]{0:T(128)} %param.9) | copy-start | bytes 388
  21.1 44.2 %copy-start.1 = (bf16[32,16384]{1,0:T(8,128)(2,1)S(1)}, bf16[32,16384]{1,0:T(8,128)(2,1)}, u32[]{:S(2)}) copy-start(bf16[32,16384]{1,0:T(8,128)(2,1)} %basis_ref.1) | copy-start | bytes 3145732

commit v9 on v8

--- a/solution.py
+++ b/solution.py
@@ -62,7 +62,7 @@
 
 def row_sums(hot, values):
     total = None
-    for _ in range(3):
+    for _ in range(2):
         part = values.astype(BF16)
         values = values - part.astype(F32)
         product = jnp.dot(hot, part, preferred_element_type=F32)
@@ -79,9 +79,10 @@
     out_ref[...] = jnp.zeros(out_ref.shape, F32)
 
 
-def state_columns(betas_ref, free_ref, temps_ref, counts_ref, start_ref, beta_cols, bias_cols):
+def state_columns(betas_ref, free_ref, temps_ref, counts_ref, start_ref, beta_cols, bias_cols, logs_ref):
     expand(state_beta(temps_ref[...], betas_ref), beta_cols, 0.0)
-    expand(log_count(counts_ref) + LOG2E * free_ref[...] + start_ref[...], bias_cols, NEG)
+    logs_ref[...] = log_count(counts_ref)
+    expand(logs_ref[...] + LOG2E * free_ref[...] + start_ref[...], bias_cols, NEG)
 
 
 def first_samples(rows_ref, cols_ref, beta_cols, bias_cols, energies_ref, out_ref, slot, total):
@@ -179,12 +180,12 @@
     copies(out_ref, log_sum(parts_ref[...]))
 
 
-def second_samples(cols_ref, values_ref, counts_ref, parts_ref, out_ref, weights_ref,
+def second_samples(cols_ref, values_ref, logs_ref, parts_ref, out_ref, weights_ref,
                    bias_cols, slot):
     cols = cols_ref[...]
     cols = [cols[0, t] for t in range(values_ref.shape[0])]
     slots = values_ref.shape[0]
-    expand(log_count(counts_ref) - log_sum(parts_ref[...]), bias_cols, NEG)
+    expand(logs_ref[...] - log_sum(parts_ref[...]), bias_cols, NEG)
     for t in range(slots):
         bias = bias_cols[cols[t]]
         for h, value in enumerate(halves(values_ref, t)):
@@ -290,7 +291,9 @@
 
     tile_rows, tile_cols, betas = (vector.reshape(1, -1) for vector in (tile_rows, tile_cols, betas))
     start = call(begin, shape(rows, LANES), [], cost=pl.CostEstimate(flops=COST, bytes_accessed=0, transcendentals=0))()
-    beta, bias = call(state_columns, (shape(*by_state), shape(*by_state)), vmem(5))(betas, free, temps, counts, start)
+    beta, bias, logs = call(state_columns, (shape(*by_state), shape(*by_state), shape(rows, LANES)), vmem(5))(
+        betas, free, temps, counts, start
+    )
     parts = call(first_samples, shape(n_state * (cut * slots + 1), LANES), vmem(5), [by_slot, by_slot])(
         tile_rows, tile_cols, beta, bias, energies
     )
@@ -315,7 +318,7 @@
         (shape(n_state, cut * slots, LANES), shape(*energies.shape)),
         vmem(4),
         [pltpu.VMEM(by_state, F32), by_slot],
-    )(tile_cols, values, counts, parts)
+    )(tile_cols, values, logs, parts)
     parts = spread(parts, "state")
     parts = call(
         second_states,

time: 107 us -> 107 us (level)
  no operation moved by 1% of the time
where the time goes in v9:
time: 107 us
  blocking collectives  99.9 us (93%)
  Pallas kernels  5.22 us (5%)
  local copies, waits for them, and re-layouts  1.73 us (2%)
    all_to_all x5, blocking collectives, spread(): return lax.all_to_all(parts, axis, 0, 0)  86.1 us
    all_gather x3, blocking collectives, pair(): return lax.all_gather(parts, 'core')  13.8 us

profile of v9, /device:TPU:1, one launch (start us, length us, event | category | flops | bytes accessed | tf_op | source)
XLA Modules:
  0.0 106.9 jit_solution(7244084422993993850)
XLA Ops:
  0.0 0.0 copy-start.6
  0.0 0.0 copy-start.7
  0.0 0.0 copy-start.5
  0.0 0.0 copy-start.4
  0.0 0.0 copy-start
  0.0 0.0 copy-start.2
  0.0 0.0 copy-start.3
  0.1 0.6 copy-done.6
  0.7 0.0 copy-done.7
  0.7 0.0 copy-done.5
  0.7 0.0 copy-done.4
  0.7 0.5 shard_map.83
  1.3 0.4 copy-done
  1.7 0.0 copy-done.2
  1.7 0.0 copy-done.3
  1.7 0.7 shard_map.84
  2.3 16.8 %all_to_all.25 = f32[16,65,1,128]{3,2,1,0:T(1,128)S(1)} all-to-all(f32[16,65,1,128]{3,2,1,0:T(1,128)S(1)} %bitcast.16), channel_id=1, replica_groups=mesh['z'=16,'core'=2,'state'=16] {'state'}, dimensions={0} | all-to-all | bytes 1064960 | tf_op jit(solution)/shard_map/all_to_all | solution.py:259
  19.1 1.9 %shard_map.85 = (f32[8,128]{1,0:T(8,128)S(1)}, f32[32,64,256]{2,1,0:T(8,128)S(1)}, bf16[64,512]{1,0:T(8,128)(2,1)S(1)}) custom-call(s32[1,32]{1,0:T(1,128)S(1)} %bitcast.24, s32[1,32]{1,0:T(1,128)S(1)} %bitcast.20, f32[17,64,128]{2,1,0:T(8,128)S(1)} %get-tuple-element.13.beta_cols, f32[32,64,256]{2,1,0:T(8,128)S(1)} %copy-done, f32[1040,128]{1,0:T(8,128)S(1)} %bitcast.15), custom_call_target="tpu_custom_call" | custom-call | tf_op jit(solution)/shard_map/pallas_call | solution.py:301
  21.1 0.0 copy-start.1
  21.1 4.9 %all-gather = f32[16,128]{1,0:T(8,128)S(1)} all-gather(f32[8,128]{1,0:T(8,128)S(1)} %get-tuple-element.17), channel_id=2, replica_groups=mesh['z'=16,'core'=2,'state'=16] {'core'}, dimensions={0}, use_global_device_ids=true | all-gather | bytes 12288 | tf_op jit(solution)/shard_map/all_gather | solution.py:263
  26.0 26.4 %all_to_all.26.parts_ref = f32[16,8,128]{2,1,0:T(8,128)S(1)} all-to-all(f32[16,8,128]{2,1,0:T(8,128)S(1)} %shard_map.86), channel_id=1, replica_groups=mesh['z'=16,'core'=2,'state'=16] {'z'}, dimensions={0} | all-to-all | bytes 131072 | tf_op jit(solution)/shard_map/all_to_all | solution.py:259
  52.4 0.8 shard_map.87
  53.2 12.0 %all_to_all.27.parts_ref = f32[16,64,128]{2,1,0:T(8,128)S(1)} all-to-all(f32[16,64,128]{2,1,0:T(8,128)S(1)} %get-tuple-element.20), channel_id=1, replica_groups=mesh['z'=16,'core'=2,'state'=16] {'state'}, dimensions={0} | all-to-all | bytes 1048576 | tf_op jit(solution)/shard_map/all_to_all | solution.py:259
  65.2 0.0 copy-done.1
  65.2 1.2 %shard_map.88 = f32[2,144,128]{2,1,0:T(8,128)S(1)} custom-call(s32[1,32]{1,0:T(1,128)S(1)} %bitcast.25, s32[1,32]{1,0:T(1,128)S(1)} %bitcast.22, f32[32,64,256]{2,1,0:T(8,128)S(1)} %get-tuple-element.18.weights_ref, bf16[64,512]{1,0:T(8,128)(2,1)S(1)} %get-tuple-element.19.hot_ref, f32[16,64,128]{2,1,0:T(8,128)S(1)} %all_to_all.27.parts_ref, ...), custom_call_target="tpu_custom_call" | custom-call | tf_op jit(solution)/shard_map/pallas_call | solution.py:323
  66.5 4.9 %all-gather.1 = f32[4,144,128]{2,1,0:T(8,128)S(1)} all-gather(f32[2,144,128]{2,1,0:T(8,128)S(1)} %shard_map.88), channel_id=3, replica_groups=mesh['z'=16,'core'=2,'state'=16] {'core'}, dimensions={0}, use_global_device_ids=true | all-gather | bytes 442368 | tf_op jit(solution)/shard_map/all_gather | solution.py:263
  71.4 15.4 %all_to_all.28.parts_ref = f32[16,9,1,128]{3,2,1,0:T(1,128)S(1)} all-to-all(f32[16,9,1,128]{3,2,1,0:T(1,128)S(1)} %shard_map.89), channel_id=1, replica_groups=mesh['z'=16,'core'=2,'state'=16] {'z'}, dimensions={0} | all-to-all | bytes 147456 | tf_op jit(solution)/shard_map/all_to_all | solution.py:259
  86.8 0.1 shard_map.90
  86.9 15.4 %all_to_all.29 = f32[16,8,128]{2,1,0:T(8,128)S(1)} all-to-all(f32[16,8,128]{2,1,0:T(8,128)S(1)} %shard_map.90), channel_id=1, replica_groups=mesh['z'=16,'core'=2,'state'=16] {'z'}, dimensions={0} | all-to-all | bytes 131072 | tf_op jit(solution)/shard_map/all_to_all | solution.py:259
  102.3 4.0 %all-gather.2 = f32[32,8,128]{2,1,0:T(8,128)S(1)} all-gather(f32[16,8,128]{2,1,0:T(8,128)S(1)} %all_to_all.29), channel_id=4, replica_groups=mesh['z'=16,'core'=2,'state'=16] {'core'}, dimensions={0}, use_global_device_ids=true | all-gather | bytes 196608 | tf_op jit(solution)/shard_map/all_gather | solution.py:263
  106.3 0.7 copy.11
  (3 shorter events, 0.0 us)
Async XLA Ops:
  0.0 0.7 copy-start.6
  0.0 0.7 copy-start.7
  0.0 0.7 copy-start.5
  0.0 0.7 copy-start.4
  0.0 1.6 %copy-start = (f32[32,64,256]{2,1,0:T(8,128)S(1)}, f32[32,64,256]{2,1,0:T(8,128)}, u32[]{:S(2)}) copy-start(f32[32,64,256]{2,1,0:T(8,128)} %energies_ref.3) | copy-start | bytes 6291460
  0.0 1.6 %copy-start.2 = (s32[32]{0:T(128)S(1)}, s32[32]{0:T(128)}, u32[]{:S(2)}) copy-start(s32[32]{0:T(128)} %param.10) | copy-start | bytes 388
  0.0 1.6 %copy-start.3 = (s32[32]{0:T(128)S(1)}, s32[32]{0:T(128)}, u32[]{:S(2)}) copy-start(s32[32]{0:T(128)} %param.9) | copy-start | bytes 388
  21.1 44.2 %copy-start.1 = (bf16[32,16384]{1,0:T(8,128)(2,1)S(1)}, bf16[32,16384]{1,0:T(8,128)(2,1)}, u32[]{:S(2)}) copy-start(bf16[32,16384]{1,0:T(8,128)(2,1)} %basis_ref.1) | copy-start | bytes 3145732
